TPU v7x, 128 devices: a whole 4x4x4 slice. The times are simulated.
128 devices in a mesh: row: 8 (over x, core), col: 16 (over y, z).
Axes of the slice: x: 4, y: 4, z: 4, core: 2. Of those that a mesh axis runs over, the one named last changes fastest.
Arguments:
- integrals: bfloat16 [8, 3, 32, 32, 6400], P('row', None, None, None, 'col'), may hold values from -2.5 to 2.5
- block_sizes: int32 [8], replicated, may hold values from 8 to 32, as said below
- int_pattern: int32 [8, 3, 64], replicated, may hold values 0 or 1
- occ_density: bfloat16 [8, 3, 32, 32], replicated, may hold values from -0.625 to 0.625
- occ_pattern: int32 [8, 3], replicated, may hold values 0 or 1
- vir_density: bfloat16 [8, 3, 32, 32], replicated, may hold values from -0.625 to 0.625
- vir_pattern: int32 [8, 3], replicated, may hold values 0 or 1
Outputs:
- response: float32 [6400, 6400], P('row', 'col')
Inputs may be any that keep to these rules, and one draw needn't show every extreme that they name: `block_sizes`: every atom block holds at least 8 functions, and some block holds exactly 32.
All inputs are finite; a program needn't handle non-finite values.
Results may differ from a plain program's by a relative error of at most 0.015.
Values may be sent and summed in bfloat16 or wider, within the bound.
A program may use at most 128 MiB of HBM per device.

v0:
```python
import jax
import jax.numpy as jnp
from jax import lax
from jax.sharding import PartitionSpec as P

BLK = 32
ND = 3
PB = 100


def with_halo(block, sides, width):
    for axis, dim in sides:
        count = lax.axis_size(axis)
        forward = [(i, i + 1) for i in range(count - 1)]
        forward.append((count - 1, 0))
        backward = [(target, source) for source, target in forward]
        low = lax.ppermute(
            lax.slice_in_dim(block, block.shape[dim] - width, None, axis=dim), axis, forward
        )
        high = lax.ppermute(lax.slice_in_dim(block, 0, width, axis=dim), axis, backward)
        block = jnp.concatenate([low, block, high], axis=dim)
    return block


def slot_masks(block_sizes):
    slot_ids = jnp.arange(BLK, dtype=jnp.int32)
    return (slot_ids[None, :] < block_sizes[:, None]).astype(jnp.bfloat16)


def masked_blocks(raw_blocks, block_index, nblocks, slot_fill, ri_fill):
    pieces = []
    for band_off in range(ND):
        partner = (block_index + band_off - 1) % nblocks
        pieces.append(
            raw_blocks[:, band_off]
            * slot_fill[block_index][:, :, None, None]
            * slot_fill[partner][:, None, :, None]
            * ri_fill[block_index, band_off][:, None, None, :]
        )
    return jnp.stack(pieces, axis=1)


def occ_side(live_ints, block_index, nblocks, occupied):
    pieces = []
    for out_band in range(ND):
        summed = None
        for mid_band in range(ND):
            step_band = out_band - mid_band + 1
            if 0 <= step_band < ND:
                density = occupied[(block_index + mid_band - 1) % nblocks, step_band]
                product = jnp.einsum(
                    "rabp,rbc->racp",
                    live_ints[:, mid_band],
                    density,
                    preferred_element_type=jnp.float32,
                )
                summed = product if summed is None else summed + product
        pieces.append(summed)
    return jnp.stack(pieces, axis=1).astype(jnp.bfloat16)


def vir_side(extended, block_index, virtual, local_rows):
    pieces = []
    for out_band in range(ND):
        summed = None
        for shift_band in range(ND):
            mid_band = out_band - shift_band + 1
            if 0 <= mid_band < ND:
                source = extended[shift_band : shift_band + local_rows, mid_band]
                product = jnp.einsum(
                    "rxa,racp->rxcp",
                    virtual[block_index, shift_band],
                    source,
                    preferred_element_type=jnp.float32,
                )
                summed = product if summed is None else summed + product
        pieces.append(summed)
    return jnp.stack(pieces, axis=1).astype(jnp.bfloat16)


def local(integrals, block_sizes, int_pattern, occ_density, occ_pattern, vir_density, vir_pattern):
    local_rows = integrals.shape[0]
    col_width = integrals.shape[4]
    row_total = lax.axis_size("row")
    nblocks = local_rows * row_total
    first_block = lax.axis_index("row") * local_rows
    own_index = first_block + jnp.arange(local_rows, dtype=jnp.int32)
    slot_fill = slot_masks(block_sizes)
    per_col = col_width // PB
    ri_local = lax.dynamic_slice_in_dim(int_pattern, lax.axis_index("col") * per_col, per_col, 2)
    ri_fill = jnp.repeat(ri_local.astype(jnp.bfloat16), PB, axis=2)
    occupied = occ_density * occ_pattern.astype(jnp.bfloat16)[:, :, None, None]
    virtual = vir_density * vir_pattern.astype(jnp.bfloat16)[:, :, None, None]
    live_ints = masked_blocks(integrals, own_index, nblocks, slot_fill, ri_fill)
    sub_width = col_width // row_total
    item_count = local_rows * ND * 2
    half_rows = BLK // 2 * BLK

    def to_items(blocks_here):
        return blocks_here.reshape(item_count, half_rows, row_total, sub_width)

    mixed_blocks = occ_side(live_ints, own_index, nblocks, occupied)
    extended = with_halo(mixed_blocks, (("row", 0),), 1)
    contracted = vir_side(extended, own_index, virtual, local_rows)
    left_items, right_items = (
        lax.all_to_all(
            lax.all_to_all(to_items(contracted), "row", split_axis=2, concat_axis=0, tiled=True),
            "col",
            split_axis=0,
            concat_axis=3,
            tiled=True,
        ),
        lax.all_to_all(
            lax.all_to_all(to_items(live_ints), "row", split_axis=2, concat_axis=0, tiled=True),
            "col",
            split_axis=0,
            concat_axis=3,
            tiled=True,
        ),
    )
    left_rows = left_items[:, :, 0, :]
    row_width = left_rows.shape[2]
    product = jnp.einsum(
        "xjp,xjsq->psq",
        left_rows,
        lax.all_gather(right_items, "row", axis=2, tiled=True),
        preferred_element_type=jnp.float32,
    )
    result = lax.psum_scatter(
        product.reshape(row_width, row_total * row_width).astype(jnp.bfloat16),
        "col",
        scatter_dimension=1,
        tiled=True,
    ).astype(jnp.float32)
    return result


def solution(mesh):
    return jax.shard_map(
        local,
        mesh=mesh,
        in_specs=(P("row", None, None, None, "col"), P(), P(), P(), P(), P(), P()),
        out_specs=P("row", "col"),
        check_vma=False,
    )
```

profile of v0, /device:TPU:0, one launch (start us, length us, event | category | flops | bytes accessed | tf_op | source)
XLA Modules:
  0.0 474.2 jit_solution(10580624926792380814)
XLA Ops:
  6.5 0.7 fusion.70
  7.3 0.8 dynamic-slice_convert_fusion
  8.3 2.3 multiply_multiply_fusion.2
  10.6 2.2 pad_maximum_fusion.2
  12.8 10.4 %reshape.260 = bf16[6,512,8,50]{3,2,1,0:T(8,128)(2,1)} reshape(bf16[1,3,32,32,400]{4,3,2,1,0:T(8,128)(2,1)} %pad_maximum_fusion.2) | data formatting | bytes 4915200 | tf_op jit(solution)/shard_map/reshape | solution.py:100
  23.2 8.1 %copy.67 = bf16[6,512,8,50]{1,3,0,2:T(8,128)(2,1)} copy(bf16[6,512,8,50]{3,2,1,0:T(8,128)(2,1)} %reshape.260) | data formatting | bytes 4915200 | tf_op jit(solution)/shard_map/reshape | solution.py:100
  31.3 39.0 %all_to_all.69 = bf16[6,512,8,50]{1,3,0,2:T(8,128)(2,1)S(1)} all-to-all(bf16[6,512,8,50]{1,3,0,2:T(8,128)(2,1)} %copy.67), channel_id=1, replica_groups=mesh['row'=8,'col'=16] {'row'}, dimensions={2} | all-to-all | bytes 4915200 | tf_op jit(solution)/shard_map/all_to_all | solution.py:114
  70.3 42.9 %all_to_all.70 = bf16[48,512,1,50]{1,3,2,0:T(8,128)(2,1)S(1)} all-to-all(bf16[48,512,1,50]{1,3,2,0:T(8,128)(2,1)S(1)} %bitcast.169), channel_id=1, replica_groups=mesh['row'=8,'col'=16] {'col'}, dimensions={0} | all-to-all | bytes 4915200 | tf_op jit(solution)/shard_map/all_to_all | solution.py:113
  113.2 1.8 copy.69
  115.0 4.2 all_to_all.64
  123.7 2.2 pad_maximum_fusion
  125.8 3.0 collective-permute-start.1
  129.0 0.9 fusion.25
  129.9 0.9 fusion.21
  130.8 0.9 fusion.15
  131.7 97.6 %collective-permute-done = bf16[1,3,32,32,400]{4,3,2,1,0:T(8,128)(2,1)} collective-permute-done((bf16[1,3,32,32,400]{4,3,2,1,0:T(8,128)(2,1)}, bf16[1,3,32,32,400]{4,3,2,1,0:T(8,128)(2,1)}, u32[]{:S(2)}, u32[]{:S(2)}) %collective-permute-start) | collective-permute-done | bytes 2457632 | tf_op jit(solution)/shard_map/ppermute | solution.py:17
  229.3 1.8 slice_bitcast_fusion.3
  231.1 0.9 fusion
  232.0 1.8 slice_bitcast_fusion.1
  233.8 0.9 fusion.1
  234.7 0.9 fusion.23
  235.6 1.0 fusion.2
  237.1 1.8 copy.63
  238.9 7.3 %convert_element_type.38 = bf16[6,512,8,50]{3,2,1,0:T(8,128)(2,1)} reshape(bf16[1,3,32,32,400]{4,3,2,1,0:T(8,128)(2,1)S(1)} %copy.63) | data formatting | bytes 4915200 | tf_op jit(solution)/shard_map/convert_element_type | solution.py:78
  246.1 7.0 %copy.64 = bf16[6,512,8,50]{1,3,0,2:T(8,128)(2,1)S(1)} copy(bf16[6,512,8,50]{3,2,1,0:T(8,128)(2,1)} %convert_element_type.38) | data formatting | bytes 4915200 | tf_op jit(solution)/shard_map/convert_element_type | solution.py:78
  253.1 38.1 %all_to_all.71 = bf16[6,512,8,50]{1,3,0,2:T(8,128)(2,1)S(1)} all-to-all(bf16[6,512,8,50]{1,3,0,2:T(8,128)(2,1)S(1)} %copy.64), channel_id=1, replica_groups=mesh['row'=8,'col'=16] {'row'}, dimensions={2} | all-to-all | bytes 4915200 | tf_op jit(solution)/shard_map/all_to_all | solution.py:107
  291.2 38.2 %all_to_all.72 = bf16[48,512,1,50]{1,3,2,0:T(8,128)(2,1)S(1)} all-to-all(bf16[48,512,1,50]{1,3,2,0:T(8,128)(2,1)S(1)} %bitcast.171), channel_id=1, replica_groups=mesh['row'=8,'col'=16] {'col'}, dimensions={0} | all-to-all | bytes 4915200 | tf_op jit(solution)/shard_map/all_to_all | solution.py:106
  329.7 2.2 squeeze.2
  332.0 9.9 %copy.70 = bf16[8,800,512,3]{2,1,0,3:T(8,128)(2,1)S(1)} copy(bf16[8,800,512,3]{2,1,3,0:T(8,128)(2,1)} %bitcast.167) | data formatting | bytes 39321600 | tf_op jit(solution)/shard_map/xjp,xjsq->psq/dot_general | solution.py:123
  341.9 23.4 %bitcast_convert_fusion = bf16[800,6400]{0,1:T(8,128)(2,1)} fusion(bf16[3,512,800]{1,2,0:T(8,128)(2,1)S(1)} %copy-done.2, bf16[6400,512,3]{1,0,2:T(8,128)(2,1)S(1)} %bitcast.168), kind=kOutput, calls=%fused_computation | convolution fusion | flops 15733760000 | bytes 32358400 | tf_op jit(solution)/shard_map/xjp,xjsq->psq/dot_general | solution.py:123
  365.4 99.6 %reduce-scatter.4.cloned.1.call-done = bf16[800,400]{0,1:T(8,128)(2,1)} async-done(((bf16[800,6400]{0,1:T(8,128)(2,1)}), bf16[800,400]{0,1:T(8,128)(2,1)}) %reduce-scatter.4.cloned.1.call-update) | async-done | bytes 640016
  465.0 2.3 convert_element_type.40
  (40 shorter events, 5.6 us)
Async XLA Ops:
  6.5 325.4 %all-gather.2.cloned.1.call-start = ((), (), s32[]{:S(2)}) async-start(), calls=%async_computation.5 | async-start | bytes 22118400 | tf_op jit(solution)/shard_map/all_gather | solution.py:126
  119.2 0.7 copy-start.5
  119.2 0.9 copy-start.3
  119.3 345.8 %reduce-scatter.4.cloned.1.call-start = ((), (), s32[]{:S(2)}) async-start(), calls=%async_computation.6 | async-start | bytes 12185600
  123.6 2.2 copy-start
  123.6 5.1 %copy-start.6 = (s32[8,3]{0,1:T(4,128)S(1)}, s32[8,3]{0,1:T(4,128)}, u32[]{:S(2)}) copy-start(s32[8,3]{0,1:T(4,128)} %param.13) | copy-start | bytes 292
  123.6 5.2 %copy-start.4 = (bf16[8,3,32,32]{3,2,1,0:T(8,128)(2,1)S(1)}, bf16[8,3,32,32]{3,2,1,0:T(8,128)(2,1)}, u32[]{:S(2)}) copy-start(bf16[8,3,32,32]{3,2,1,0:T(8,128)(2,1)} %param.12) | copy-start | bytes 147460
  125.8 103.5 %collective-permute-start = (bf16[1,3,32,32,400]{4,3,2,1,0:T(8,128)(2,1)}, bf16[1,3,32,32,400]{4,3,2,1,0:T(8,128)(2,1)}, u32[]{:S(2)}, u32[]{:S(2)}) collective-permute-start(bf16[1,3,32,32,400]{4,3,2,1,0:T(8,128)(2,1)} %pad_maximum_fusion), channel_id=1, source_target_pairs={{0,16},{16,32},{32,48},{48,64},{64,80},{80,96},{96,112},{112,0},{1... | collective-permute-start | bytes 7372808 | tf_op jit(solution)/shard_map/ppermute | solution.py:17
  125.8 4.1 copy-start.1
  125.8 106.2 %collective-permute-start.1 = (bf16[1,3,32,32,400]{4,3,2,1,0:T(8,128)(2,1)}, bf16[1,3,32,32,400]{4,3,2,1,0:T(8,128)(2,1)}, u32[]{:S(2)}, u32[]{:S(2)}) collective-permute-start(bf16[1,3,32,32,400]{4,3,2,1,0:T(8,128)(2,1)} %pad_maximum_fusion), channel_id=1, source_target_pairs={{16,0},{32,16},{48,32},{64,48},{80,64},{96,80},{112,96},{0,112},{1... | collective-permute-start | bytes 7372808 | tf_op jit(solution)/shard_map/ppermute | solution.py:20
  332.0 10.0 %copy-start.2 = (bf16[3,512,800]{1,2,0:T(8,128)(2,1)S(1)}, bf16[3,512,800]{1,2,0:T(8,128)(2,1)}, u32[]{:S(2)}) copy-start(bf16[3,512,800]{1,2,0:T(8,128)(2,1)} %squeeze.2) | copy-start | bytes 7372804
Sparse Core Ops, SparseCore 0:
  119.4 125.8 all-gather.1
  365.5 99.4 reduce-scatter.3
where the time goes:
time: 475 us; the launch traced here: 474 us
  waiting for transfers between devices  197 us (41%)
  blocking collectives  158 us (33%)
  local copies, waits for them, and re-layouts  57.6 us (12%)
  matrix products  33.2 us (7%)
  between operations  13.6 us (3%)
  other arithmetic  11.1 us (2%)
    unnamed x3, waiting for transfers between devices  99.7 us
    ppermute x1, waiting for transfers between devices, with_halo(): lax.ppermute(lax.slice_in_dim(block, block.shape[dim] - width, None, axis...  97.6 us
    all_to_all x1, blocking collectives, local(): lax.all_to_all(lax.all_to_all(to_items(live_ints), 'row', split_axis=2, c...  42.9 us
    all_to_all x1, blocking collectives, local(): lax.all_to_all(to_items(live_ints), 'row', split_axis=2, concat_axis=0, t...  39 us
    all_to_all x1, blocking collectives, local(): lax.all_to_all(lax.all_to_all(to_items(contracted), 'row', split_axis=2,...  38.2 us
    all_to_all x1, blocking collectives, local(): lax.all_to_all(to_items(contracted), 'row', split_axis=2, concat_axis=0,...  38.1 us
    dot_general x1, matrix products, local(): jnp.einsum('xjp,xjsq->psq', left_rows, lax.all_gather(right_items, 'row',...  23.4 us
    reshape x2, local copies, waits for them, and re-layouts, to_items(): return blocks_here.reshape(item_count, half_rows, row_total, sub_width)  18.6 us
  transfers between devices with their start and end apart: 4, of which 2 were waited for; matrix products, arithmetic and copies ran while one was open for 7% of the time, Pallas kernels for 0%

commit v1 on v0

v1 whole, which is shorter than its diff:
```python
import jax
import jax.numpy as jnp
from jax import lax
from jax.experimental import pallas as pl
from jax.experimental.pallas import tpu as pltpu
from jax.sharding import PartitionSpec as P

BLK = 32
ND = 3
PB = 100
NB = 8
NX = 4
W = 400
SUB = 50
SLOT = 64
PIECE = 512
NPIECE = 6
LANES = 256
QOFF = (0, 400, 800, 1280)
QROWS = 1792
MESH = pl.DeviceIdType.MESH
NT = (((1,), (1,)), ((), ()))
NN = (((1,), (0,)), ((), ()))
GROUPS = (
    ((0,), 0, 1280, (0, 1, 2)),
    ((1, 2), 0, 1280, (0, 1, 2)),
    ((0, 1, 2), 1280, 512, (3,)),
    ((3,), 0, 1792, (0, 1, 2, 3)),
)


def iota(shape, dim):
    return lax.broadcasted_iota(jnp.int32, shape, dim)


def dot(a, b, dims=NN):
    return lax.dot_general(a, b, dims, preferred_element_type=jnp.float32)


def wrap(v, n=NX):
    return lax.rem(v + n, n)


def kernel(
    sizes, ri, occ_pat, vir_pat, ints, occ, vir, out,
    right, left, mixed, halo, occ_mat, vir_mat, acc, fin, one_hot, msgs, got,
    s0, s1, s2, s3, d0, d1, d2, d3, x0, x1, x2, x3,
    r_send, r_recv, l_send, l_recv, h_send, h_recv, c_send, c_recv, x_send, x_recv, a_send, a_recv,
):
    parts, cores, hops = (s0, s1, s2, s3), (d0, d1, d2, d3), (x0, x1, x2, x3)
    row = lax.axis_index("row")
    col = lax.axis_index("col")
    x, k = row // 2, lax.rem(row, 2)
    y, z = col // NX, lax.rem(col, NX)
    bf = jnp.bfloat16

    def at(nx, nk, ny, nz):
        return (2 * nx + nk, NX * ny + nz)

    up_x, down_x, far_x = wrap(x + 1), wrap(x - 1), wrap(x + 2)
    y_dev = (at(x, k, wrap(y + 1), z), at(x, k, wrap(y - 1), z))
    z_dev = (at(x, k, y, wrap(z + 1)), at(x, k, y, wrap(z - 1)))
    x_dev = (at(up_x, k, y, z), at(down_x, k, y, z))
    h_dev = ((wrap(row + 1, NB), col), (wrap(row - 1, NB), col))
    other = at(x, 1 - k, y, z)
    far_halo = (wrap(row + 2 * k - 1, NB), col)

    barrier = pltpu.get_barrier_semaphore()
    for target in (x_dev[0], x_dev[1], other, far_halo):
        pl.semaphore_signal(barrier, inc=1, device_id=target, device_id_type=MESH)

    def greet(n, _):
        target = (row, NX * wrap(y + n // NX) + wrap(z + lax.rem(n, NX)))
        pl.semaphore_signal(barrier, inc=1, device_id=target, device_id_type=MESH)
        return 0

    lax.fori_loop(1, NX * NX, greet, 0)

    def remote(src, dst, send, recv, target):
        return pltpu.make_async_remote_copy(
            src_ref=src, dst_ref=dst, send_sem=send, recv_sem=recv, device_id=target, device_id_type=MESH
        )

    own_size = sizes[row]
    eye = iota((W, W), 0) == iota((W, W), 1)
    ri_block = iota((1, W), 1) // PB

    def turn(p, _):
        e = p // 2
        keep = jnp.zeros((1, W), jnp.float32)
        for q in range(W // PB):
            value = ri[row, e, NX * col + q].astype(jnp.float32)
            keep = jnp.where(ri_block == q, value, keep)
        diag = jnp.where(eye, keep, 0.0).astype(bf)
        lane = iota((1, PIECE), 1) + lax.rem(p, 2) * PIECE
        partner = sizes[wrap(row + e - 1, NB)]
        fill = jnp.where((lane // BLK < own_size) & (lane % BLK < partner), 1.0, 0.0)
        rows = ints[e, pl.ds(pl.multiple_of(lax.rem(p, 2) * PIECE, PIECE), PIECE), :]
        right[p, 0:W, :] = (dot(diag, rows, NT) * fill).astype(bf)
        return 0

    lax.fori_loop(0, NPIECE, turn, 0)
    pl.semaphore_wait(barrier, NX * NX - 1 + 4)

    def gather_copies(view, send, recv, targets):
        own, onward = {}, {}
        for way in (0, 1):
            for p in range(NPIECE):
                own[way, p] = remote(
                    view(p, 0), view(p, 1 + way), send.at[way, p], recv.at[way, p], targets[way]
                )
            for j in range(ND):
                p = 2 * j + way
                onward[way, j] = remote(
                    view(p, 1 + way), view(p, 3), send.at[way, NPIECE + j], recv.at[way, NPIECE + j], targets[way]
                )
        return own, onward

    def right_view(p, slot):
        return right.at[p, pl.ds(QOFF[slot], W), :]

    def left_view(p, slot):
        return left.at[p, slot]

    r_own, r_on = gather_copies(right_view, r_send, r_recv, y_dev)
    l_own, l_on = gather_copies(left_view, l_send, l_recv, z_dev)
    for p in range(NPIECE):
        for way in (0, 1):
            r_own[way, p].start()

    inner = (iota((LANES, BLK), 0) % BLK == iota((LANES, BLK), 1)).astype(bf)
    same = iota((LANES, LANES), 0) // BLK == iota((LANES, LANES), 1) // BLK

    def spread_occ(n, _):
        e, f = n // ND, lax.rem(n, ND)
        j = wrap(row + e - 1, NB)
        block = (occ[j, f].astype(jnp.float32) * occ_pat[j, f].astype(jnp.float32)).astype(bf)
        wide = dot(dot(inner, block).astype(bf), inner, NT)
        occ_mat[n] = jnp.where(same, wide, 0.0).astype(bf)
        return 0

    lax.fori_loop(0, ND * ND, spread_occ, 0)

    halos = {}
    for way, order in ((0, (1, 2)), (1, (1, 0))):
        for j, band in enumerate(order):
            halos[way, j] = remote(
                mixed.at[band], halo.at[2 * way + j], h_send.at[way, j], h_recv.at[way, j], h_dev[way]
            )

    def mix(dm):
        def body(g, _):
            h, start = g // 2, pl.multiple_of(lax.rem(g, 2) * LANES, LANES)
            total = None
            for e in range(ND):
                f = dm + 1 - e
                if 0 <= f < ND:
                    term = dot(right[2 * e + h, 0:W, pl.ds(start, LANES)], occ_mat[ND * e + f])
                    total = term if total is None else total + term
            mixed[dm, :, pl.ds(pl.multiple_of(g * LANES, LANES), LANES)] = total.astype(bf)
            return 0

        lax.fori_loop(0, BLK * BLK // LANES, body, 0)

    mix(1)
    halos[0, 0].start()
    halos[1, 0].start()
    mix(2)
    halos[0, 1].start()
    mix(0)
    halos[1, 1].start()

    def spread_vir(n, _):
        g, part = n // NX, lax.rem(n, NX)
        block = (vir[row, g].astype(jnp.float32) * vir_pat[row, g].astype(jnp.float32)).astype(bf)
        outer = (iota((BLK * BLK, BLK), 0) // BLK == iota((BLK * BLK, BLK), 1)).astype(bf)
        tall = dot(outer, block, NT).astype(bf)
        columns = iota((LANES, BLK), 0) + part * LANES
        wide = dot(tall, (columns // BLK == iota((LANES, BLK), 1)).astype(bf), NT)
        match = iota((BLK * BLK, LANES), 0) % BLK == iota((BLK * BLK, LANES), 1) % BLK
        vir_mat[g, :, pl.ds(pl.multiple_of(part * LANES, LANES), LANES)] = jnp.where(match, wide, 0.0).astype(bf)
        return 0

    lax.fori_loop(0, ND * NX, spread_vir, 0)

    def contract(d, terms):
        def body(h, _):
            columns = pl.ds(pl.multiple_of(h * PIECE, PIECE), PIECE)
            total = None
            for ref, index, g in terms:
                term = dot(ref[index], vir_mat[g, :, columns])
                total = term if total is None else total + term
            left[2 * d + h, 0] = total.astype(bf)
            return 0

        lax.fori_loop(0, 2, body, 0)
        for h in (0, 1):
            for way in (0, 1):
                l_own[way, 2 * d + h].start()

    halos[0, 0].wait_recv()
    contract(0, ((halo, 0, 0), (mixed, 0, 1)))
    halos[1, 0].wait_recv()
    contract(2, ((mixed, 2, 1), (halo, 2, 2)))
    halos[0, 1].wait_recv()
    halos[1, 1].wait_recv()
    contract(1, ((halo, 1, 0), (mixed, 1, 1), (halo, 3, 2)))
    l_order = (0, 1, 4, 5, 2, 3)

    for yy in (0, 1):
        source = iota((W, 8 * 128), 0)
        target = iota((W, 8 * 128), 1)
        hit = (source // SUB == target // 128) & (target % 128 == yy * SUB + source % SUB)
        one_hot[yy] = jnp.where(hit, 1.0, 0.0).astype(bf)
    for p in range(NPIECE):
        right[p, 1200:1280, :] = jnp.zeros((80, PIECE), bf)
        right[p, 1680:1792, :] = jnp.zeros((112, PIECE), bf)
    acc[W:, :] = jnp.zeros((acc.shape[0] - W, acc.shape[1]), jnp.float32)

    def product(slot, first, lanes, pieces=tuple(range(NPIECE)), add=False):
        def body(n, _):
            start = pl.multiple_of(n * LANES, LANES)
            q_rows = pl.ds(pl.multiple_of(first + n * LANES, LANES), LANES)
            total = acc[0:W, pl.ds(start, LANES)] if add else None
            for p in pieces:
                term = dot(left[p, slot], right[p, q_rows, :], NT)
                total = term if total is None else total + term
            acc[0:W, pl.ds(start, LANES)] = total
            return 0

        lax.fori_loop(0, lanes // LANES, body, 0)

    def split(n, which):
        lanes = GROUPS[n][2]
        for s in range(8):
            parts[n][s % 2, s // 2, which] = acc[SUB * s : SUB * s + SLOT, 0:lanes].astype(bf)

    core_copy, hop_copy = {}, {}

    def core_start(n):
        core_copy[n] = remote(parts[n].at[1 - k], cores[n], c_send.at[n], c_recv.at[n], other)
        core_copy[n].start()

    half = SLOT // 2
    low, high = pl.ds(0, half), pl.ds(half, half)

    def hop(n, way, m, src):
        hop_copy[n, way, m] = remote(
            src, hops[n].at[way, m], x_send.at[n, way, m], x_recv.at[n, way, m], x_dev[way]
        )
        hop_copy[n, way, m].start()

    def stage1(n):
        ref, extra = parts[n], cores[n]
        core_copy[n].wait_recv()
        mine = ref.at[k]

        def join(b):
            mine[b] = (mine[b].astype(jnp.float32) + extra[b].astype(jnp.float32)).astype(bf)

        join(far_x)
        hop(n, 0, 0, mine.at[far_x, :, low, :])
        hop(n, 1, 0, mine.at[far_x, :, high, :])
        join(up_x)
        hop(n, 0, 1, mine.at[up_x, :, high, :])
        join(down_x)
        hop(n, 1, 1, mine.at[down_x, :, low, :])
        join(x)

    def stage2(n):
        mine = parts[n].at[k]
        for way, b, rows in ((0, up_x, low), (1, down_x, high)):
            hop_copy[n, way, 0].wait_recv()
            mine[b, :, rows, :] = (
                mine[b, :, rows, :].astype(jnp.float32) + hops[n][way, 0].astype(jnp.float32)
            ).astype(bf)
            hop(n, way, 2, mine.at[b, :, rows, :])

    def stage3(n):
        slots, _, _, q_slots = GROUPS[n]
        mine = parts[n].at[k]
        for way in (0, 1):
            for m in (1, 2):
                hop_copy[n, way, m].wait_recv()
        for rows, one, two in ((low, 2, 1), (high, 1, 2)):
            total = (
                mine[x, :, rows, :].astype(jnp.float32)
                + hops[n][0, one].astype(jnp.float32)
                + hops[n][1, two].astype(jnp.float32)
            )
            for i, slot in enumerate(slots):
                for q in q_slots:
                    lane = QOFF[q] - GROUPS[n][1]
                    there = wrap(y + (0, -1, 1, 2)[q])
                    fin[slot, there, rows, :] = total[i, :, lane : lane + W].astype(bf)

    exchange = {}

    def exchange_start(n, slots):
        for slot in slots:
            for pair in (0, 1):
                packed = (dot(fin[slot, 2 * pair], one_hot[0]) + dot(fin[slot, 2 * pair + 1], one_hot[1])).astype(bf)
                for s in range(8):
                    target = NX * (s // 2) + 2 * (s % 2) + pair
                    msgs[target, slot] = packed[:, 128 * s : 128 * s + 128]
        which = pl.ds(slots[0], len(slots))

        def copy(m):
            target = NX * wrap(y + m // NX) + wrap(z + lax.rem(m, NX))
            return remote(
                msgs.at[target, which], got.at[col, which], a_send.at[n, m - 1], a_recv.at[n, m - 1], (row, target)
            )

        exchange[n] = copy

        def begin(m, _):
            copy(m).start()
            return 0

        lax.fori_loop(1, NX * NX, begin, 0)
        for slot in slots:
            got[col, slot] = msgs[col, slot]

    def exchange_wait(n, what):
        def body(m, _):
            if what == "recv":
                exchange[n](m).wait_recv()
            else:
                exchange[n](m).wait_send()
            return 0

        lax.fori_loop(1, NX * NX, body, 0)

    for p in range(NPIECE):
        for way in (0, 1):
            r_own[way, p].wait_recv()
            if p % 2 == way:
                r_on[way, p // 2].start()
    product(0, 0, 1280)
    split(0, 0)
    core_start(0)
    for p in l_order:
        for way in (0, 1):
            l_own[way, p].wait_recv()
            if p % 2 == way:
                l_on[way, p // 2].start()
    stage1(0)
    product(1, 0, 1280)
    split(1, 0)
    product(2, 0, 1280)
    split(1, 1)
    core_start(1)
    stage2(0)
    for j in range(ND):
        for way in (0, 1):
            r_on[way, j].wait_recv()
    stage1(1)
    stage3(0)
    for i, slot in enumerate((0, 1, 2)):
        product(slot, 1280, 512)
        split(2, i)
    core_start(2)
    stage2(1)
    steps = [lambda: stage1(2), lambda: stage3(1), lambda: stage2(2), lambda: stage3(2)]
    seen = 0
    for j in (0, 2, 1):
        for way in (0, 1):
            l_on[way, j].wait_recv()
            product(3, 0, 1792, (2 * j + way,), add=seen > 0)
            seen += 1
            if steps and seen >= 1 and seen <= 4:
                steps.pop(0)()
    split(3, 0)
    core_start(3)
    exchange_start(0, (0, 1, 2))
    stage1(3)
    stage2(3)
    stage3(3)
    exchange_start(1, (3,))

    source = iota((4 * 128, W), 0)
    target = iota((4 * 128, W), 1)
    inside = source % 128
    place = jnp.where(
        (inside < 2 * SUB) & (target == (4 * (inside // SUB) + source // 128) * SUB + inside % SUB), 1.0, 0.0
    ).astype(bf)
    exchange_wait(0, "recv")
    exchange_wait(1, "recv")
    slot_of = {0: 0, 3: 1, 1: 2, 2: 3}
    for yy in range(NX):
        for zz in range(NX):
            pieces = [got[NX * yy + src, slot_of[(zz - src) % NX]] for src in range(NX)]
            block = dot(jnp.concatenate(pieces, axis=1), place)
            start = (NX * yy + zz) * SUB
            out[start : start + SUB, :] = block[0:SUB]

    for copies in (r_own, r_on, l_own, l_on, halos, core_copy, hop_copy):
        for copy in copies.values():
            copy.wait_send()
    exchange_wait(0, "send")
    exchange_wait(1, "send")


def local(integrals, block_sizes, int_pattern, occ_density, occ_pattern, vir_density, vir_pattern):
    ints = integrals.reshape(ND, BLK * BLK, W)
    bf = jnp.bfloat16
    vmem = pl.BlockSpec(memory_space=pltpu.VMEM)
    smem = pl.BlockSpec(memory_space=pltpu.SMEM)
    dma = pltpu.SemaphoreType.DMA
    group_shapes = [(len(g[0]), g[2]) for g in GROUPS]
    scratch = [
        pltpu.VMEM((NPIECE, QROWS, PIECE), bf),
        pltpu.VMEM((NPIECE, NX, W, PIECE), bf),
        pltpu.VMEM((ND, W, BLK * BLK), bf),
        pltpu.VMEM((4, W, BLK * BLK), bf),
        pltpu.VMEM((ND * ND, LANES, LANES), bf),
        pltpu.VMEM((ND, BLK * BLK, BLK * BLK), bf),
        pltpu.VMEM((416, QROWS), jnp.float32),
        pltpu.VMEM((NX, NX, SLOT, W), bf),
        pltpu.VMEM((2, W, 8 * 128), bf),
        pltpu.VMEM((NX * NX, NX, SLOT, 128), bf),
        pltpu.VMEM((NX * NX, NX, SLOT, 128), bf),
        *[pltpu.VMEM((2, NX, n, SLOT, lanes), bf) for n, lanes in group_shapes],
        *[pltpu.VMEM((NX, n, SLOT, lanes), bf) for n, lanes in group_shapes],
        *[pltpu.VMEM((2, 3, n, SLOT // 2, lanes), bf) for n, lanes in group_shapes],
        dma((2, NPIECE + ND)), dma((2, NPIECE + ND)),
        dma((2, NPIECE + ND)), dma((2, NPIECE + ND)),
        dma((2, 2)), dma((2, 2)),
        dma((4,)), dma((4,)),
        dma((4, 2, 3)), dma((4, 2, 3)),
        dma((2, NX * NX - 1)), dma((2, NX * NX - 1)),
    ]
    return pl.pallas_call(
        kernel,
        out_shape=jax.ShapeDtypeStruct((800, W), jnp.float32),
        in_specs=[smem, smem, smem, smem, vmem, vmem, vmem],
        out_specs=vmem,
        scratch_shapes=scratch,
        compiler_params=pltpu.CompilerParams(
            collective_id=0, has_side_effects=True, vmem_limit_bytes=64 * 1024 * 1024
        ),
    )(block_sizes, int_pattern, occ_pattern, vir_pattern, ints, occ_density, vir_density)


def solution(mesh):
    return jax.shard_map(
        local,
        mesh=mesh,
        in_specs=(P("row", None, None, None, "col"), P(), P(), P(), P(), P(), P()),
        out_specs=P("row", "col"),
        check_vma=False,
    )
```

time: 475 us -> 149 us (0.31)
  waiting for transfers between devices: 197 us -> 0 us
  blocking collectives: 158 us -> 0 us
  Pallas kernels: 0 us -> 142 us
  local copies, waits for them, and re-layouts: 57.6 us -> 7.04 us
  matrix products: 33.2 us -> 0 us
  between operations: 13.6 us -> 0.01 us
  other arithmetic: 11.1 us -> 0 us
    all_to_all x4 -> x0, blocking collectives: 158 us -> none  [the longest x1 42.9 us: local(): lax.all_to_all(lax.all_to_all(to_items(live_ints), 'row', split_axis=2, c...]
    pallas_call x0 -> x1, Pallas kernels: none -> 142 us  [local(): pl.pallas_call(kernel, out_shape=jax.ShapeDtypeStruct((800, W), jnp.float...]
    unnamed x3 -> x0, waiting for transfers between devices: 99.7 us -> none
    ppermute x2 -> x0, waiting for transfers between devices: 97.6 us -> none  [the longest x1 97.6 us: with_halo(): lax.ppermute(lax.slice_in_dim(block, block.shape[dim] - width, None, axis...]
    dot_general x15 -> x0, matrix products: 33.2 us -> none  [the longest x1 23.4 us: local(): jnp.einsum('xjp,xjsq->psq', left_rows, lax.all_gather(right_items, 'row',...]
    reshape x3 -> x0, local copies, waits for them, and re-layouts: 18.6 us -> none  [the longest x2 18.6 us: to_items(): return blocks_here.reshape(item_count, half_rows, row_total, sub_width)]
    convert_element_type x4 -> x0, local copies, waits for them, and re-layouts: 14.5 us -> none  [the longest x2 14.3 us: vir_side(): return jnp.stack(pieces, axis=1).astype(jnp.bfloat16)]
    dot_general x1 -> x0, local copies, waits for them, and re-layouts: 9.94 us -> none  [local(): jnp.einsum('xjp,xjsq->psq', left_rows, lax.all_gather(right_items, 'row',...]
  transfers between devices with their start and end apart: 4 -> 0, of which waited for: 2 -> 0; matrix products, arithmetic and copies ran while one was open for 7% -> 0% of each run, Pallas kernels for 0% -> 0%
where the time goes in v1:
time: 149 us
  Pallas kernels  142 us (95%)
  local copies, waits for them, and re-layouts  7.04 us (5%)
    pallas_call x1, Pallas kernels, local(): pl.pallas_call(kernel, out_shape=jax.ShapeDtypeStruct((800, W), jnp.float...  142 us
    unnamed x3, local copies, waits for them, and re-layouts  4 us
    pallas_call x1, local copies, waits for them, and re-layouts, local(): pl.pallas_call(kernel, out_shape=jax.ShapeDtypeStruct((800, W), jnp.float...  3.04 us

profile of v1, /device:TPU:0, one launch (start us, length us, event | category | flops | bytes accessed | tf_op | source)
XLA Modules:
  0.0 149.0 jit_solution(4240888583243482925)
XLA Ops:
  0.0 1.3 copy.9.occ_pat
  1.3 1.3 copy.10.vir_pat
  2.7 1.3 copy.8.ri
  4.0 141.9 %shard_map.73 = f32[800,400]{1,0:T(8,128)} custom-call(s32[8]{0:T(128)} %sizes.1, s32[8,3,64]{2,1,0:T(4,128)} %copy.8.ri, s32[8,3]{1,0:T(8,128)} %copy.9.occ_pat, s32[8,3]{1,0:T(8,128)} %copy.10.vir_pat, bf16[3,1024,400]{2,1,0:T(8,128)(2,1)} %bitcast.1, bf16[8,3,32,32]{3,2,1,0:T(8,128)(2,1)} %occ.1, bf16[8,3,32,32]{3,2,1,0:T(8,128)(2,1)} %vir.1), custom_call_target="tpu_custom_call" | custom-call | tf_op jit(solution)/shard_map/pallas_call | solution.py:433
  145.9 3.0 %copy.11 = f32[800,400]{0,1:T(8,128)} copy(f32[800,400]{1,0:T(8,128)} %shard_map.73) | data formatting | bytes 2560000 | tf_op jit(solution)/shard_map/pallas_call | solution.py:433

commit v2 on v1

v2 whole, which is shorter than its diff:
```python
import jax
import jax.numpy as jnp
from jax import lax
from jax.experimental import pallas as pl
from jax.experimental.pallas import tpu as pltpu
from jax.sharding import PartitionSpec as P

BLK = 32
ND = 3
PB = 100
NB = 8
NX = 4
W = 400
SUB = 50
SLOT = 64
PIECE = 512
NPIECE = 6
LANES = 256
PARTS = (12, 12, 12, 14)
BASE = (0, 96, 192, 288)
PART_ROWS = (96, 96, 96, 112)
TILE = 16
QOFF = (0, 400, 800)
QFAR = (1280, 1376, 1536, 1632)
QROWS = 1792
MESH = pl.DeviceIdType.MESH
NT = (((1,), (1,)), ((), ()))
NN = (((1,), (0,)), ((), ()))
NEAR = ((0, 0, 0, 400), (1, 400, 0, 400), (2, 800, 0, 400))
FAR_A, FAR_B = (3, 1280, 0, 192), (3, 1536, 192, 208)
ALL = (0, 1, 2, 3)
GROUPS = (
    ((0,), ALL, 0, 1280, NEAR),
    ((1, 2), ALL, 0, 1280, NEAR),
    ((0, 1, 2), ALL, 1280, 256, (FAR_A,)),
    ((0, 1, 2), ALL, 1536, 256, (FAR_B,)),
    ((3,), (0, 1), 0, 1792, (*NEAR, FAR_A, FAR_B)),
    ((3,), (2, 3), 0, 1792, (*NEAR, FAR_A, FAR_B)),
)
NG = len(GROUPS)


def iota(shape, dim):
    return lax.broadcasted_iota(jnp.int32, shape, dim)


def dot(a, b, dims=NN):
    return lax.dot_general(a, b, dims, preferred_element_type=jnp.float32)


def function_of(v):
    part = (v >= BASE[1]).astype(jnp.int32) + (v >= BASE[2]).astype(jnp.int32) + (v >= BASE[3]).astype(jnp.int32)
    rest = v - BASE[1] * part
    owner = jnp.where(part == 3, rest // PARTS[3], rest // PARTS[0])
    return owner, PARTS[0] * part + rest - owner * jnp.where(part == 3, PARTS[3], PARTS[0])


def wrap(v, n=NX):
    return lax.rem(v + n, n)


def kernel(sizes, ri, occ_pat, vir_pat, ints_hbm, occ, vir, out, *scratch):
    ints, right, left, mixed, halo, occ_mat, vir_mat, match, acc, fin, one_hot, place, choose, wide, msgs, got = scratch[:16]
    parts, cores, hops = scratch[16 : 16 + NG], scratch[16 + NG : 16 + 2 * NG], scratch[16 + 2 * NG : 16 + 3 * NG]
    (
        i_sem, r_send, r_recv, rf_send, rf_recv, l_send, l_recv, lf_send, lf_recv,
        h_send, h_recv, c_send, c_recv, x_send, x_recv, a_send, a_recv,
    ) = scratch[16 + 3 * NG :]
    row = lax.axis_index("row")
    col = lax.axis_index("col")
    x, k = row // 2, lax.rem(row, 2)
    y, z = col // NX, lax.rem(col, NX)
    bf = jnp.bfloat16

    def at(nx, nk, ny, nz):
        return (2 * nx + nk, NX * ny + nz)

    up_x, down_x, far_x = wrap(x + 1), wrap(x - 1), wrap(x + 2)
    y_dev = (at(x, k, wrap(y + 1), z), at(x, k, wrap(y - 1), z))
    z_dev = (at(x, k, y, wrap(z + 1)), at(x, k, y, wrap(z - 1)))
    x_dev = (at(up_x, k, y, z), at(down_x, k, y, z))
    other = at(x, 1 - k, y, z)
    far_halo = (wrap(row + 2 * k - 1, NB), col)

    barrier = pltpu.get_barrier_semaphore()
    for target in (other, far_halo, *x_dev):
        pl.semaphore_signal(barrier, inc=1, device_id=target, device_id_type=MESH)

    def greet(n, _):
        target = (row, NX * wrap(y + n // NX) + wrap(z + lax.rem(n, NX)))
        pl.semaphore_signal(barrier, inc=1, device_id=target, device_id_type=MESH)
        return 0

    lax.fori_loop(1, NX * NX, greet, 0)
    loads = [pltpu.make_async_copy(ints_hbm.at[e], ints.at[e], i_sem.at[e]) for e in range(ND)]
    for load in loads:
        load.start()

    def remote(src, dst, send, recv, target):
        return pltpu.make_async_remote_copy(
            src_ref=src, dst_ref=dst, send_sem=send, recv_sem=recv, device_id=target, device_id_type=MESH
        )

    inner = ((iota((LANES, BLK), 0) & 31) == iota((LANES, BLK), 1)).astype(bf)
    same = (iota((LANES, LANES), 0) >> 5) == (iota((LANES, LANES), 1) >> 5)

    def spread_occ(n, _):
        e, f = n // ND, lax.rem(n, ND)
        j = wrap(row + e - 1, NB)
        block = (occ[j, f].astype(jnp.float32) * occ_pat[f, j].astype(jnp.float32)).astype(bf)
        full = dot(dot(inner, block).astype(bf), inner, NT)
        occ_mat[n] = jnp.where(same, full, 0.0).astype(bf)
        return 0

    lax.fori_loop(0, ND * ND, spread_occ, 0)

    own_size = sizes[row]
    owner, function = function_of(iota((W, 1), 0))
    eye = iota((W, W), 1) == owner * SUB + function
    ri_block = iota((1, W), 1) // PB

    def turn(p, _):
        e = p // 2
        keep = jnp.zeros((1, W), jnp.float32)
        for q in range(W // PB):
            value = ri[e, row, (W // PB) * col + q].astype(jnp.float32)
            keep = jnp.where(ri_block == q, value, keep)
        diag = jnp.where(eye, keep, 0.0).astype(bf)
        lane = iota((1, PIECE), 1) + lax.rem(p, 2) * PIECE
        partner = sizes[wrap(row + e - 1, NB)]
        fill = jnp.where(((lane >> 5) < own_size) & ((lane & 31) < partner), 1.0, 0.0)
        rows = ints[e, pl.ds(pl.multiple_of(lax.rem(p, 2) * PIECE, PIECE), PIECE), :]
        right[p, 0:W, :] = (dot(diag, rows, NT) * fill).astype(bf)
        return 0

    for e in range(ND):
        loads[e].wait()
        lax.fori_loop(2 * e, 2 * e + 2, turn, 0)
    pl.semaphore_wait(barrier, NX * NX - 1 + 4)

    def gather_copies(view, far, sems, targets):
        send, recv, on_send, on_recv = sems
        own, onward = {}, {}
        for way in (0, 1):
            for p in range(NPIECE):
                own[way, p] = remote(
                    view(p, 1, 0, 0, W), view(p, 1, 1 + way, 0, W), send.at[way, p], recv.at[way, p], targets[way]
                )
            for late in (0, 1):
                part = 2 * late + way
                for band in range(ND):
                    onward[way, late, band] = remote(
                        view(2 * band, 2, 1 + way, BASE[part], PART_ROWS[part]),
                        far(2 * band, 2, part),
                        on_send.at[way, late, band],
                        on_recv.at[way, late, band],
                        targets[way],
                    )
        return own, onward

    def right_view(p, n, slot, first, rows):
        return right.at[pl.ds(p, n), pl.ds(QOFF[slot] + first, rows), :]

    def right_far(p, n, part):
        return right.at[pl.ds(p, n), pl.ds(QFAR[part], PART_ROWS[part]), :]

    def left_view(p, n, slot, first, rows):
        return left.at[pl.ds(p, n), slot, pl.ds(first, rows), :]

    def left_far(p, n, part):
        return left_view(p, n, 3, BASE[part], PART_ROWS[part])

    r_own, r_on = gather_copies(right_view, right_far, (r_send, r_recv, rf_send, rf_recv), y_dev)
    l_own, l_on = gather_copies(left_view, left_far, (l_send, l_recv, lf_send, lf_recv), z_dev)
    for p in range(NPIECE):
        for way in (0, 1):
            r_own[way, p].start()

    near, far = 2 - 2 * k, 2 * k
    halos = {}
    for n, (band, target) in enumerate(((1, other), (near, other), (1, far_halo), (far, far_halo))):
        halos[n] = remote(mixed.at[band], halo.at[n], h_send.at[n], h_recv.at[n], target)

    def mix(dm, pairs):
        def body(g, _):
            h, start = g // 2, pl.multiple_of(lax.rem(g, 2) * LANES, LANES)
            total = None
            for e, f in pairs:
                term = dot(right[2 * e + h, 0:W, pl.ds(start, LANES)], occ_mat[ND * e + f])
                total = term if total is None else total + term
            mixed[dm, :, pl.ds(pl.multiple_of(g * LANES, LANES), LANES)] = total.astype(bf)
            return 0

        lax.fori_loop(0, BLK * BLK // LANES, body, 0)

    mix(1, ((0, 2), (1, 1), (2, 0)))
    halos[0].start()
    halos[2].start()
    mix(near, ((near // 2, near + 1 - near // 2), (near // 2 + 1, near - near // 2)))
    halos[1].start()
    mix(far, ((far // 2, far + 1 - far // 2), (far // 2 + 1, far - far // 2)))
    halos[3].start()

    match[...] = jnp.where((iota(match.shape, 0) & 31) == (iota(match.shape, 1) & 31), 1.0, 0.0).astype(bf)
    outer = ((iota((BLK * BLK, BLK), 0) >> 5) == iota((BLK * BLK, BLK), 1)).astype(bf)

    def spread_vir(g):
        block = (vir[row, g].astype(jnp.float32) * vir_pat[g, row].astype(jnp.float32)).astype(bf)
        tall = dot(outer, block, NT).astype(bf)

        def body(part, _):
            columns = iota((LANES, BLK), 0) + part * LANES
            full = dot(tall, ((columns >> 5) == iota((LANES, BLK), 1)).astype(bf), NT)
            vir_mat[g, :, pl.ds(pl.multiple_of(part * LANES, LANES), LANES)] = full.astype(bf) * match[...]
            return 0

        lax.fori_loop(0, BLK * BLK // LANES, body, 0)

    def contract(order, terms):
        def body(h, _):
            columns = pl.ds(pl.multiple_of(h * PIECE, PIECE), PIECE)
            total = None
            for ref, index, g in terms:
                term = dot(ref[index], vir_mat[g, :, columns])
                total = term if total is None else total + term
            left[2 * order + h, 0] = total.astype(bf)
            return 0

        lax.fori_loop(0, 2, body, 0)
        for h in (0, 1):
            for way in (0, 1):
                l_own[way, 2 * order + h].start()

    bands = (near, far, 1)
    spread_vir(1)
    spread_vir(near)
    halos[0].wait_recv()
    contract(0, ((mixed, near, 1), (halo, 0, near)))
    spread_vir(far)
    halos[2].wait_recv()
    contract(1, ((mixed, far, 1), (halo, 2, far)))
    halos[1].wait_recv()
    halos[3].wait_recv()
    contract(2, ((mixed, 1, 1), (halo, 1, near), (halo, 3, far)))

    for yy in (0, 1):
        owner, function = function_of(iota((W, 1), 0))
        target = iota((W, 8 * 128), 1)
        one_hot[yy] = jnp.where(target == owner * 128 + yy * SUB + function, 1.0, 0.0).astype(bf)
    lane = iota((1, NX * 128), 1)
    inside = lane & 127
    late = (inside >= SUB).astype(jnp.int32)
    column = (4 * late + (lane >> 7)) * SUB + inside - SUB * late
    place[...] = jnp.where((inside < 2 * SUB) & (iota(place.shape, 0) == column), 1.0, 0.0).astype(bf)
    source = iota((NX * NX * SLOT, 1), 0)
    part = (source >> 4) & 3
    inside = source & 15
    target = (source >> 6) * SUB + PARTS[0] * part + inside
    real = inside < jnp.where(part == 3, PARTS[3], PARTS[0])
    choose[...] = jnp.where(real & (iota(choose.shape, 1) == target), 1.0, 0.0).astype(bf)
    for p in range(NPIECE):
        right[p, 1200:1280, :] = jnp.zeros((80, PIECE), bf)
        right[p, 1472:1536, :] = jnp.zeros((64, PIECE), bf)
        right[p, 1744:1792, :] = jnp.zeros((48, PIECE), bf)
    acc[W:, :] = jnp.zeros((acc.shape[0] - W, acc.shape[1]), jnp.float32)

    def product(slot, first, lanes, rows=(0, W), orders=(0, 1, 2), add=False):
        p_rows = pl.ds(rows[0], rows[1] - rows[0])

        def body(n, _):
            start = pl.multiple_of(n * LANES, LANES)
            q_rows = pl.ds(pl.multiple_of(first + n * LANES, LANES), LANES)
            total = acc[p_rows, pl.ds(start, LANES)] if add else None
            for order in orders:
                for h in (0, 1):
                    term = dot(left[2 * order + h, slot, p_rows, :], right[2 * bands[order] + h, q_rows, :], NT)
                    total = term if total is None else total + term
            acc[p_rows, pl.ds(start, LANES)] = total
            return 0

        lax.fori_loop(0, lanes // LANES, body, 0)

    def split(n, which):
        _, some, _, lanes, _ = GROUPS[n]
        for s in range(8):
            for i, part in enumerate(some):
                first = BASE[part] + s * PARTS[part]
                parts[n][s % 2, s // 2, which, TILE * i : TILE * i + TILE] = acc[first : first + TILE, 0:lanes].astype(bf)

    core_copy, hop_copy = {}, {}

    def core_start(n):
        core_copy[n] = remote(parts[n].at[1 - k], cores[n], c_send.at[n], c_recv.at[n], other)
        core_copy[n].start()

    def halves(n):
        half = TILE * len(GROUPS[n][1]) // 2
        return pl.ds(0, half), pl.ds(half, half)

    def hop(n, way, m, src):
        hop_copy[n, way, m] = remote(
            src, hops[n].at[way, m], x_send.at[n, way, m], x_recv.at[n, way, m], x_dev[way]
        )
        hop_copy[n, way, m].start()

    def stage1(n):
        ref, extra = parts[n], cores[n]
        low, high = halves(n)
        core_copy[n].wait_recv()
        mine = ref.at[k]

        def join(b):
            mine[b] = (mine[b].astype(jnp.float32) + extra[b].astype(jnp.float32)).astype(bf)

        join(far_x)
        hop(n, 0, 0, mine.at[far_x, :, low, :])
        hop(n, 1, 0, mine.at[far_x, :, high, :])
        join(up_x)
        hop(n, 0, 1, mine.at[up_x, :, high, :])
        join(down_x)
        hop(n, 1, 1, mine.at[down_x, :, low, :])
        join(x)

    def stage2(n):
        mine = parts[n].at[k]
        low, high = halves(n)
        for way, b, rows in ((0, up_x, low), (1, down_x, high)):
            hop_copy[n, way, 0].wait_recv()
            mine[b, :, rows, :] = (
                mine[b, :, rows, :].astype(jnp.float32) + hops[n][way, 0].astype(jnp.float32)
            ).astype(bf)
            hop(n, way, 2, mine.at[b, :, rows, :])

    def stage3(n):
        slots, some, first, _, q_pieces = GROUPS[n]
        mine = parts[n].at[k]
        low, high = halves(n)
        half = TILE * len(some) // 2
        for way in (0, 1):
            for m in (1, 2):
                hop_copy[n, way, m].wait_recv()
        for rows, one, two, start in ((low, 2, 1, 0), (high, 1, 2, half)):
            total = (
                mine[x, :, rows, :].astype(jnp.float32)
                + hops[n][0, one].astype(jnp.float32)
                + hops[n][1, two].astype(jnp.float32)
            )
            start += TILE * some[0]
            for i, slot in enumerate(slots):
                for q, lane, into, width in q_pieces:
                    there = wrap(y + (0, -1, 1, 2)[q])
                    block = total[i, :, lane - first : lane - first + width].astype(bf)
                    fin[slot, there, start : start + half, into : into + width] = block

    exchange = {}

    def exchange_start(n, slots, rows):
        rows = pl.ds(*rows)
        for slot in slots:
            for pair in (0, 1):
                low, high = fin[slot, 2 * pair, rows, :], fin[slot, 2 * pair + 1, rows, :]
                packed = (dot(low, one_hot[0]) + dot(high, one_hot[1])).astype(bf)
                for s in range(8):
                    target = NX * (s // 2) + 2 * (s % 2) + pair
                    msgs[target, slot, rows, :] = packed[:, 128 * s : 128 * s + 128]
        which = pl.ds(slots[0], len(slots))

        def copy(m):
            target = NX * wrap(y + m // NX) + wrap(z + lax.rem(m, NX))
            return remote(
                msgs.at[target, which, rows, :],
                got.at[col, which, rows, :],
                a_send.at[n, m - 1],
                a_recv.at[n, m - 1],
                (row, target),
            )

        exchange[n] = copy

        def begin(m, _):
            copy(m).start()
            return 0

        lax.fori_loop(1, NX * NX, begin, 0)
        for slot in slots:
            got[col, slot, rows, :] = msgs[col, slot, rows, :]

    def exchange_wait(n, what):
        def body(m, _):
            if what == "recv":
                exchange[n](m).wait_recv()
            else:
                exchange[n](m).wait_send()
            return 0

        lax.fori_loop(1, NX * NX, body, 0)

    def arrive(order, own, onward):
        for band in order:
            for way in (0, 1):
                own[way, 2 * band].wait_recv()
                own[way, 2 * band + 1].wait_recv()
                onward[way, 0, band].start()
        for band in order:
            for way in (0, 1):
                onward[way, 1, band].start()

    def far_arrive(onward, late, order):
        for band in order:
            for way in (0, 1):
                onward[way, late, band].wait_recv()

    every = (0, 1, 2)
    arrive(every, r_own, r_on)
    product(0, 0, 1280)
    split(0, 0)
    core_start(0)
    arrive(every, l_own, l_on)
    stage1(0)
    product(1, 0, 1280)
    split(1, 0)
    product(2, 0, 1280)
    split(1, 1)
    core_start(1)
    stage2(0)
    far_arrive(r_on, 0, every)
    for i, slot in enumerate(every):
        product(slot, 1280, 256)
        split(2, i)
    core_start(2)
    stage1(1)
    stage3(0)
    stage2(1)
    stage1(2)
    far_arrive(l_on, 0, every)
    stage3(1)
    stage2(2)
    far_arrive(r_on, 1, every)
    for i, slot in enumerate(every):
        product(slot, 1536, 256)
        split(3, i)
    core_start(3)
    early, late = (0, BASE[2]), (BASE[2], W)
    product(3, 0, 1792, early)
    split(4, 0)
    core_start(4)
    stage3(2)
    stage1(3)
    far_arrive(l_on, 1, (0,))
    product(3, 0, 1792, late, (0,))
    stage1(4)
    stage2(3)
    far_arrive(l_on, 1, (1,))
    product(3, 0, 1792, late, (1,), True)
    stage2(4)
    far_arrive(l_on, 1, (2,))
    product(3, 0, 1792, late, (2,), True)
    split(5, 0)
    core_start(5)
    stage3(3)
    exchange_start(0, every, (0, SLOT))
    stage1(5)
    stage3(4)
    exchange_start(1, (3,), (0, SLOT // 2))
    stage2(5)
    stage3(5)
    exchange_start(2, (3,), (SLOT // 2, SLOT // 2))

    for n in range(3):
        exchange_wait(n, "recv")
    slot_of = {0: 0, 3: 1, 1: 2, 2: 3}
    for yy in range(NX):
        rows = [
            jnp.concatenate([got[NX * yy + src, slot_of[(zz - src) % NX]] for src in range(NX)], axis=1)
            for zz in range(NX)
        ]
        wide[:, 256 * yy : 256 * yy + 256] = dot(place[...], jnp.concatenate(rows, axis=0), NT).astype(bf)
    out[...] = dot(wide[...], choose[...])

    for copies in (r_own, r_on, l_own, l_on, halos, core_copy, hop_copy):
        for copy in copies.values():
            copy.wait_send()
    for n in range(3):
        exchange_wait(n, "send")


def local(integrals, block_sizes, int_pattern, occ_density, occ_pattern, vir_density, vir_pattern):
    ints = integrals.reshape(ND, BLK * BLK, W)
    bf = jnp.bfloat16
    vmem = pl.BlockSpec(memory_space=pltpu.VMEM)
    smem = pl.BlockSpec(memory_space=pltpu.SMEM)
    dma = pltpu.SemaphoreType.DMA
    shapes = [(len(slots), TILE * len(some), lanes) for slots, some, _, lanes, _ in GROUPS]
    scratch = [
        pltpu.VMEM((ND, BLK * BLK, W), bf),
        pltpu.VMEM((NPIECE, QROWS, PIECE), bf),
        pltpu.VMEM((NPIECE, NX, W, PIECE), bf),
        pltpu.VMEM((ND, W, BLK * BLK), bf),
        pltpu.VMEM((4, W, BLK * BLK), bf),
        pltpu.VMEM((ND * ND, LANES, LANES), bf),
        pltpu.VMEM((ND, BLK * BLK, BLK * BLK), bf),
        pltpu.VMEM((BLK * BLK, LANES), bf),
        pltpu.VMEM((416, QROWS), jnp.float32),
        pltpu.VMEM((NX, NX, SLOT, W), bf),
        pltpu.VMEM((2, W, 8 * 128), bf),
        pltpu.VMEM((W, NX * 128), bf),
        pltpu.VMEM((NX * NX * SLOT, 800), bf),
        pltpu.VMEM((W, NX * NX * SLOT), bf),
        pltpu.VMEM((NX * NX, NX, SLOT, 128), bf),
        pltpu.VMEM((NX * NX, NX, SLOT, 128), bf),
        *[pltpu.VMEM((2, NX, n, rows, lanes), bf) for n, rows, lanes in shapes],
        *[pltpu.VMEM((NX, n, rows, lanes), bf) for n, rows, lanes in shapes],
        *[pltpu.VMEM((2, 3, n, rows // 2, lanes), bf) for n, rows, lanes in shapes],
        dma((ND,)),
        *[dma((2, NPIECE)), dma((2, NPIECE)), dma((2, 2, ND)), dma((2, 2, ND))] * 2,
        dma((4,)), dma((4,)),
        dma((NG,)), dma((NG,)),
        dma((NG, 2, 3)), dma((NG, 2, 3)),
        dma((3, NX * NX - 1)), dma((3, NX * NX - 1)),
    ]
    response = pl.pallas_call(
        kernel,
        out_shape=jax.ShapeDtypeStruct((W, 800), jnp.float32),
        in_specs=[smem, smem, smem, smem, pl.BlockSpec(memory_space=pl.ANY), vmem, vmem],
        out_specs=vmem,
        scratch_shapes=scratch,
        compiler_params=pltpu.CompilerParams(
            collective_id=0, has_side_effects=True, vmem_limit_bytes=64 * 1024 * 1024
        ),
    )(block_sizes, int_pattern.transpose(1, 0, 2), occ_pattern.T, vir_pattern.T, ints, occ_density, vir_density)
    return response.T


def solution(mesh):
    return jax.shard_map(
        local,
        mesh=mesh,
        in_specs=(P("row", None, None, None, "col"), P(), P(), P(), P(), P(), P()),
        out_specs=P("row", "col"),
        check_vma=False,
    )
```

time: 149 us -> 143 us (0.960)
  local copies, waits for them, and re-layouts: 7.04 us -> 2.55 us
  Pallas kernels: 142 us -> 140 us
    pallas_call x1 -> x0, local copies, waits for them, and re-layouts: 3.04 us -> none  [local(): pl.pallas_call(kernel, out_shape=jax.ShapeDtypeStruct((800, W), jnp.float...]
    pallas_call x1, Pallas kernels: 142 us -> 140 us  [local(): pl.pallas_call(kernel, out_shape=jax.ShapeDtypeStruct((W, 800), jnp.float...]
    unnamed x3 -> x1, local copies, waits for them, and re-layouts: 4 us -> 2.55 us
where the time goes in v2:
time: 143 us
  Pallas kernels  140 us (98%)
  local copies, waits for them, and re-layouts  2.55 us (2%)
    pallas_call x1, Pallas kernels, local(): pl.pallas_call(kernel, out_shape=jax.ShapeDtypeStruct((W, 800), jnp.float...  140 us

profile of v2, /device:TPU:0, one launch (start us, length us, event | category | flops | bytes accessed | tf_op | source)
XLA Modules:
  0.0 142.5 jit_solution(13330232936386464876)
XLA Ops:
  0.0 140.0 %shard_map.73 = f32[400,800]{1,0:T(8,128)} custom-call(s32[8]{0:T(128)} %sizes.1, s32[3,8,64]{2,1,0:T(8,128)} %bitcast.7, s32[3,8]{1,0:T(4,128)} %bitcast.8, s32[3,8]{1,0:T(4,128)} %bitcast.9, bf16[3,1024,400]{2,1,0:T(8,128)(2,1)} %bitcast.6, bf16[8,3,32,32]{3,2,1,0:T(8,128)(2,1)} %occ.1, bf16[8,3,32,32]{3,2,1,0:T(8,128)(2,1)} %vir.1), custom_call_target="tpu_custom_call" | custom-call | tf_op jit(solution)/shard_map/pallas_call | solution.py:521
  140.0 2.5 %copy.9 = f32[800,400]{0,1:T(8,128)} copy(f32[800,400]{0,1:T(8,128)} %bitcast.5) | data formatting | bytes 2560000

commit v3 on v2

--- a/solution.py
+++ b/solution.py
@@ -31,7 +31,8 @@
 ALL = (0, 1, 2, 3)
 GROUPS = (
     ((0,), ALL, 0, 1280, NEAR),
-    ((1, 2), ALL, 0, 1280, NEAR),
+    ((1,), ALL, 0, 1280, NEAR),
+    ((2,), ALL, 0, 1280, NEAR),
     ((0, 1, 2), ALL, 1280, 256, (FAR_A,)),
     ((0, 1, 2), ALL, 1536, 256, (FAR_B,)),
     ((3,), (0, 1), 0, 1792, (*NEAR, FAR_A, FAR_B)),
@@ -60,12 +61,12 @@
 
 
 def kernel(sizes, ri, occ_pat, vir_pat, ints_hbm, occ, vir, out, *scratch):
-    ints, right, left, mixed, halo, occ_mat, vir_mat, match, acc, fin, one_hot, place, choose, wide, msgs, got = scratch[:16]
-    parts, cores, hops = scratch[16 : 16 + NG], scratch[16 + NG : 16 + 2 * NG], scratch[16 + 2 * NG : 16 + 3 * NG]
+    ints, right, left, mixed, halo, occ_mat, vir_mat, match, tall, acc, fin, one_hot, place, choose, wide, msgs, got = scratch[:17]
+    parts, cores, hops = scratch[17 : 17 + NG], scratch[17 + NG : 17 + 2 * NG], scratch[17 + 2 * NG : 17 + 3 * NG]
     (
         i_sem, r_send, r_recv, rf_send, rf_recv, l_send, l_recv, lf_send, lf_recv,
-        h_send, h_recv, c_send, c_recv, x_send, x_recv, a_send, a_recv,
-    ) = scratch[16 + 3 * NG :]
+        h_send, h_recv, c_send, c_recv, x_send, x_recv, a_send, a_recv, meet,
+    ) = scratch[17 + 3 * NG :]
     row = lax.axis_index("row")
     col = lax.axis_index("col")
     x, k = row // 2, lax.rem(row, 2)
@@ -83,15 +84,8 @@
     far_halo = (wrap(row + 2 * k - 1, NB), col)
 
     barrier = pltpu.get_barrier_semaphore()
-    for target in (other, far_halo, *x_dev):
+    for target in (other, far_halo, *y_dev, *z_dev, *x_dev):
         pl.semaphore_signal(barrier, inc=1, device_id=target, device_id_type=MESH)
-
-    def greet(n, _):
-        target = (row, NX * wrap(y + n // NX) + wrap(z + lax.rem(n, NX)))
-        pl.semaphore_signal(barrier, inc=1, device_id=target, device_id_type=MESH)
-        return 0
-
-    lax.fori_loop(1, NX * NX, greet, 0)
     loads = [pltpu.make_async_copy(ints_hbm.at[e], ints.at[e], i_sem.at[e]) for e in range(ND)]
     for load in loads:
         load.start()
@@ -112,7 +106,7 @@
         occ_mat[n] = jnp.where(same, full, 0.0).astype(bf)
         return 0
 
-    lax.fori_loop(0, ND * ND, spread_occ, 0)
+    lax.fori_loop(0, ND, lambda n, c: spread_occ(2 * n + 2, c), 0)
 
     own_size = sizes[row]
     owner, function = function_of(iota((W, 1), 0))
@@ -136,7 +130,16 @@
     for e in range(ND):
         loads[e].wait()
         lax.fori_loop(2 * e, 2 * e + 2, turn, 0)
-    pl.semaphore_wait(barrier, NX * NX - 1 + 4)
+    pl.semaphore_wait(barrier, 8)
+
+    def meet_signal(n, targets):
+        for target in targets:
+            pl.semaphore_signal(meet.at[n], inc=1, device_id=target, device_id_type=MESH)
+
+    def meet_wait(n):
+        pl.semaphore_wait(meet.at[n], 2)
+
+    meet_signal(0, y_dev)
 
     def gather_copies(view, far, sems, targets):
         send, recv, on_send, on_recv = sems
@@ -196,25 +199,25 @@
     mix(1, ((0, 2), (1, 1), (2, 0)))
     halos[0].start()
     halos[2].start()
+    lax.fori_loop(0, 4, lambda n, c: spread_occ(2 * n + 1, c), 0)
     mix(near, ((near // 2, near + 1 - near // 2), (near // 2 + 1, near - near // 2)))
     halos[1].start()
     mix(far, ((far // 2, far + 1 - far // 2), (far // 2 + 1, far - far // 2)))
     halos[3].start()
 
-    match[...] = jnp.where((iota(match.shape, 0) & 31) == (iota(match.shape, 1) & 31), 1.0, 0.0).astype(bf)
-    outer = ((iota((BLK * BLK, BLK), 0) >> 5) == iota((BLK * BLK, BLK), 1)).astype(bf)
+    match[...] = jnp.where(iota(match.shape, 0) == (iota(match.shape, 1) & 31), 1.0, 0.0)
+    repeat = ((iota((BLK, BLK * BLK), 1) >> 5) == iota((BLK, BLK * BLK), 0)).astype(bf)
 
     def spread_vir(g):
         block = (vir[row, g].astype(jnp.float32) * vir_pat[g, row].astype(jnp.float32)).astype(bf)
-        tall = dot(outer, block, NT).astype(bf)
-
-        def body(part, _):
-            columns = iota((LANES, BLK), 0) + part * LANES
-            full = dot(tall, ((columns >> 5) == iota((LANES, BLK), 1)).astype(bf), NT)
-            vir_mat[g, :, pl.ds(pl.multiple_of(part * LANES, LANES), LANES)] = full.astype(bf) * match[...]
+        tall[...] = dot(block, repeat, (((0,), (0,)), ((), ())))
+
+        def body(a, _):
+            rows = tall[pl.ds(a, 1), :] * match[...]
+            vir_mat[g, pl.ds(pl.multiple_of(a * BLK, BLK), BLK), :] = rows.astype(bf)
             return 0
 
-        lax.fori_loop(0, BLK * BLK // LANES, body, 0)
+        lax.fori_loop(0, BLK, body, 0)
 
     def contract(order, terms):
         def body(h, _):
@@ -231,6 +234,8 @@
             for way in (0, 1):
                 l_own[way, 2 * order + h].start()
 
+    meet_wait(0)
+    meet_signal(1, z_dev)
     bands = (near, far, 1)
     spread_vir(1)
     spread_vir(near)
@@ -264,11 +269,11 @@
         right[p, 1744:1792, :] = jnp.zeros((48, PIECE), bf)
     acc[W:, :] = jnp.zeros((acc.shape[0] - W, acc.shape[1]), jnp.float32)
 
-    def product(slot, first, lanes, rows=(0, W), orders=(0, 1, 2), add=False):
+    def product(slot, first, lanes, rows=(0, W), orders=(0, 1, 2), add=False, into=0):
         p_rows = pl.ds(rows[0], rows[1] - rows[0])
 
         def body(n, _):
-            start = pl.multiple_of(n * LANES, LANES)
+            start = pl.multiple_of(into + n * LANES, LANES)
             q_rows = pl.ds(pl.multiple_of(first + n * LANES, LANES), LANES)
             total = acc[p_rows, pl.ds(start, LANES)] if add else None
             for order in orders:
@@ -280,12 +285,12 @@
 
         lax.fori_loop(0, lanes // LANES, body, 0)
 
-    def split(n, which):
+    def split(n, which, lane=0):
         _, some, _, lanes, _ = GROUPS[n]
         for s in range(8):
             for i, part in enumerate(some):
                 first = BASE[part] + s * PARTS[part]
-                parts[n][s % 2, s // 2, which, TILE * i : TILE * i + TILE] = acc[first : first + TILE, 0:lanes].astype(bf)
+                parts[n][s % 2, s // 2, which, TILE * i : TILE * i + TILE] = acc[first : first + TILE, lane : lane + lanes].astype(bf)
 
     core_copy, hop_copy = {}, {}
 
@@ -350,29 +355,23 @@
                 for q, lane, into, width in q_pieces:
                     there = wrap(y + (0, -1, 1, 2)[q])
                     block = total[i, :, lane - first : lane - first + width].astype(bf)
-                    fin[slot, there, start : start + half, into : into + width] = block
+                    fin[there, SLOT * slot + start : SLOT * slot + start + half, into : into + width] = block
 
     exchange = {}
 
-    def exchange_start(n, slots, rows):
-        rows = pl.ds(*rows)
-        for slot in slots:
-            for pair in (0, 1):
-                low, high = fin[slot, 2 * pair, rows, :], fin[slot, 2 * pair + 1, rows, :]
-                packed = (dot(low, one_hot[0]) + dot(high, one_hot[1])).astype(bf)
-                for s in range(8):
-                    target = NX * (s // 2) + 2 * (s % 2) + pair
-                    msgs[target, slot, rows, :] = packed[:, 128 * s : 128 * s + 128]
-        which = pl.ds(slots[0], len(slots))
+    def exchange_start(n, slots):
+        rows = pl.ds(SLOT * slots[0], SLOT * len(slots))
+        for pair in (0, 1):
+            packed = dot(fin[2 * pair, rows, :], one_hot[0]) + dot(fin[2 * pair + 1, rows, :], one_hot[1])
+            packed = packed.astype(bf)
+            for s in range(8):
+                target = NX * (s // 2) + 2 * (s % 2) + pair
+                msgs[target, rows, :] = packed[:, 128 * s : 128 * s + 128]
 
         def copy(m):
             target = NX * wrap(y + m // NX) + wrap(z + lax.rem(m, NX))
             return remote(
-                msgs.at[target, which, rows, :],
-                got.at[col, which, rows, :],
-                a_send.at[n, m - 1],
-                a_recv.at[n, m - 1],
-                (row, target),
+                msgs.at[target, rows, :], got.at[col, rows, :], a_send.at[n, m - 1], a_recv.at[n, m - 1], (row, target)
             )
 
         exchange[n] = copy
@@ -382,8 +381,7 @@
             return 0
 
         lax.fori_loop(1, NX * NX, begin, 0)
-        for slot in slots:
-            got[col, slot, rows, :] = msgs[col, slot, rows, :]
+        got[col, rows, :] = msgs[col, rows, :]
 
     def exchange_wait(n, what):
         def body(m, _):
@@ -415,72 +413,79 @@
     product(0, 0, 1280)
     split(0, 0)
     core_start(0)
+    meet_wait(1)
+    meet_signal(2, z_dev)
+    stage1(0)
     arrive(every, l_own, l_on)
-    stage1(0)
     product(1, 0, 1280)
     split(1, 0)
-    product(2, 0, 1280)
-    split(1, 1)
     core_start(1)
     stage2(0)
+    product(2, 0, 1280)
+    split(2, 0)
+    core_start(2)
+    stage1(1)
+    meet_wait(2)
     far_arrive(r_on, 0, every)
     for i, slot in enumerate(every):
         product(slot, 1280, 256)
-        split(2, i)
-    core_start(2)
-    stage1(1)
-    stage3(0)
-    stage2(1)
-    stage1(2)
-    far_arrive(l_on, 0, every)
-    stage3(1)
-    stage2(2)
-    far_arrive(r_on, 1, every)
-    for i, slot in enumerate(every):
-        product(slot, 1536, 256)
         split(3, i)
     core_start(3)
+    stage1(2)
+    stage2(1)
+    stage3(0)
     early, late = (0, BASE[2]), (BASE[2], W)
-    product(3, 0, 1792, early)
-    split(4, 0)
+    stage1(3)
+    stage2(2)
+    far_arrive(l_on, 0, every)
+    product(3, 0, 1536, early)
+    stage3(1)
+    stage2(3)
+    far_arrive(r_on, 1, every)
+    product(3, 1536, 256, early, into=1536)
+    split(5, 0)
+    core_start(5)
+    for i, slot in enumerate(every):
+        product(slot, 1536, 256, into=1536)
+        split(4, i, 1536)
     core_start(4)
+    stage1(5)
     stage3(2)
-    stage1(3)
     far_arrive(l_on, 1, (0,))
     product(3, 0, 1792, late, (0,))
     stage1(4)
-    stage2(3)
+    stage3(3)
+    stage2(5)
     far_arrive(l_on, 1, (1,))
     product(3, 0, 1792, late, (1,), True)
     stage2(4)
     far_arrive(l_on, 1, (2,))
     product(3, 0, 1792, late, (2,), True)
-    split(5, 0)
-    core_start(5)
-    stage3(3)
-    exchange_start(0, every, (0, SLOT))
-    stage1(5)
+    split(6, 0)
+    core_start(6)
+    stage3(5)
     stage3(4)
-    exchange_start(1, (3,), (0, SLOT // 2))
-    stage2(5)
-    stage3(5)
-    exchange_start(2, (3,), (SLOT // 2, SLOT // 2))
-
-    for n in range(3):
+    stage1(6)
+    exchange_start(0, every)
+    stage2(6)
+    stage3(6)
+    exchange_start(1, (3,))
+
+    for n in (0, 1):
         exchange_wait(n, "recv")
     slot_of = {0: 0, 3: 1, 1: 2, 2: 3}
     for yy in range(NX):
         rows = [
-            jnp.concatenate([got[NX * yy + src, slot_of[(zz - src) % NX]] for src in range(NX)], axis=1)
+            jnp.concatenate([got[NX * yy + src, pl.ds(SLOT * slot_of[(zz - src) % NX], SLOT)] for src in range(NX)], axis=1)
             for zz in range(NX)
         ]
         wide[:, 256 * yy : 256 * yy + 256] = dot(place[...], jnp.concatenate(rows, axis=0), NT).astype(bf)
-    out[...] = dot(wide[...], choose[...])
+    out[...] = dot(wide[...], choose[...]).astype(bf)
 
     for copies in (r_own, r_on, l_own, l_on, halos, core_copy, hop_copy):
         for copy in copies.values():
             copy.wait_send()
-    for n in range(3):
+    for n in (0, 1):
         exchange_wait(n, "send")
 
 
@@ -499,15 +504,16 @@
         pltpu.VMEM((4, W, BLK * BLK), bf),
         pltpu.VMEM((ND * ND, LANES, LANES), bf),
         pltpu.VMEM((ND, BLK * BLK, BLK * BLK), bf),
-        pltpu.VMEM((BLK * BLK, LANES), bf),
+        pltpu.VMEM((BLK, BLK * BLK), jnp.float32),
+        pltpu.VMEM((BLK, BLK * BLK), jnp.float32),
         pltpu.VMEM((416, QROWS), jnp.float32),
-        pltpu.VMEM((NX, NX, SLOT, W), bf),
+        pltpu.VMEM((NX, NX * SLOT, W), bf),
         pltpu.VMEM((2, W, 8 * 128), bf),
         pltpu.VMEM((W, NX * 128), bf),
         pltpu.VMEM((NX * NX * SLOT, 800), bf),
         pltpu.VMEM((W, NX * NX * SLOT), bf),
-        pltpu.VMEM((NX * NX, NX, SLOT, 128), bf),
-        pltpu.VMEM((NX * NX, NX, SLOT, 128), bf),
+        pltpu.VMEM((NX * NX, NX * SLOT, 128), bf),
+        pltpu.VMEM((NX * NX, NX * SLOT, 128), bf),
         *[pltpu.VMEM((2, NX, n, rows, lanes), bf) for n, rows, lanes in shapes],
         *[pltpu.VMEM((NX, n, rows, lanes), bf) for n, rows, lanes in shapes],
         *[pltpu.VMEM((2, 3, n, rows // 2, lanes), bf) for n, rows, lanes in shapes],
@@ -516,11 +522,12 @@
         dma((4,)), dma((4,)),
         dma((NG,)), dma((NG,)),
         dma((NG, 2, 3)), dma((NG, 2, 3)),
-        dma((3, NX * NX - 1)), dma((3, NX * NX - 1)),
+        dma((2, NX * NX - 1)), dma((2, NX * NX - 1)),
+        pltpu.SemaphoreType.REGULAR((3,)),
     ]
     response = pl.pallas_call(
         kernel,
-        out_shape=jax.ShapeDtypeStruct((W, 800), jnp.float32),
+        out_shape=jax.ShapeDtypeStruct((W, 800), bf),
         in_specs=[smem, smem, smem, smem, pl.BlockSpec(memory_space=pl.ANY), vmem, vmem],
         out_specs=vmem,
         scratch_shapes=scratch,
@@ -528,7 +535,7 @@
             collective_id=0, has_side_effects=True, vmem_limit_bytes=64 * 1024 * 1024
         ),
     )(block_sizes, int_pattern.transpose(1, 0, 2), occ_pattern.T, vir_pattern.T, ints, occ_density, vir_density)
-    return response.T
+    return response.astype(jnp.float32).T
 
 
 def solution(mesh):

time: 143 us -> 132 us (0.923)
  Pallas kernels: 140 us -> 129 us
  local copies, waits for them, and re-layouts: 2.55 us -> 0 us
  other arithmetic: 0 us -> 2.3 us
    pallas_call x1, Pallas kernels: 140 us -> 129 us  [local(): pl.pallas_call(kernel, out_shape=jax.ShapeDtypeStruct((W, 800), bf), in_s...]
    unnamed x1 -> x0, local copies, waits for them, and re-layouts: 2.55 us -> none
    transpose x0 -> x1, other arithmetic: none -> 2.3 us  [local(): return response.astype(jnp.float32).T]
where the time goes in v3:
time: 132 us
  Pallas kernels  129 us (98%)
  other arithmetic  2.3 us (2%)
    pallas_call x1, Pallas kernels, local(): pl.pallas_call(kernel, out_shape=jax.ShapeDtypeStruct((W, 800), bf), in_s...  129 us

profile of v3, /device:TPU:0, one launch (start us, length us, event | category | flops | bytes accessed | tf_op | source)
XLA Modules:
  0.0 131.6 jit_solution(990512030456767885)
XLA Ops:
  0.0 129.3 %shard_map.73 = bf16[400,800]{1,0:T(8,128)(2,1)} custom-call(s32[8]{0:T(128)} %sizes.1, s32[3,8,64]{2,1,0:T(8,128)} %bitcast.7, s32[3,8]{1,0:T(4,128)} %bitcast.8, s32[3,8]{1,0:T(4,128)} %bitcast.9, bf16[3,1024,400]{2,1,0:T(8,128)(2,1)} %bitcast.6, bf16[8,3,32,32]{3,2,1,0:T(8,128)(2,1)} %occ.1, bf16[8,3,32,32]{3,2,1,0:T(8,128)(2,1)} %vir.1), custom_call_target="tpu_custom_call" | custom-call | tf_op jit(solution)/shard_map/pallas_call | solution.py:528
  129.3 2.3 %convert_bitcast_fusion = f32[800,400]{0,1:T(8,128)} fusion(bf16[400,800]{1,0:T(8,128)(2,1)} %shard_map.73), kind=kLoop, calls=%fused_computation | loop fusion | flops 320000 | bytes 1920000 | tf_op jit(solution)/shard_map/transpose | solution.py:538

commit v4 on v3

--- a/solution.py
+++ b/solution.py
@@ -39,6 +39,7 @@
     ((3,), (2, 3), 0, 1792, (*NEAR, FAR_A, FAR_B)),
 )
 NG = len(GROUPS)
+PLACES = ((0, 0), (0, 1), (1, 1), (1, 2), (2, 2), (2, 3), (3, 3))
 
 
 def iota(shape, dim):
@@ -61,7 +62,7 @@
 
 
 def kernel(sizes, ri, occ_pat, vir_pat, ints_hbm, occ, vir, out, *scratch):
-    ints, right, left, mixed, halo, occ_mat, vir_mat, match, tall, acc, fin, one_hot, place, choose, wide, msgs, got = scratch[:17]
+    ints, right, left, mixed, halo, occ_mat, vir_mat, match, tall, acc, near_acc, fin, one_hot, place, choose, msgs, got = scratch[:17]
     parts, cores, hops = scratch[17 : 17 + NG], scratch[17 + NG : 17 + 2 * NG], scratch[17 + 2 * NG : 17 + 3 * NG]
     (
         i_sem, r_send, r_recv, rf_send, rf_recv, l_send, l_recv, lf_send, lf_recv,
@@ -83,11 +84,16 @@
     other = at(x, 1 - k, y, z)
     far_halo = (wrap(row + 2 * k - 1, NB), col)
 
+    near, far = 2 - 2 * k, 2 * k
+    bands = (near, far, 1)
     barrier = pltpu.get_barrier_semaphore()
     for target in (other, far_halo, *y_dev, *z_dev, *x_dev):
         pl.semaphore_signal(barrier, inc=1, device_id=target, device_id_type=MESH)
-    loads = [pltpu.make_async_copy(ints_hbm.at[e], ints.at[e], i_sem.at[e]) for e in range(ND)]
-    for load in loads:
+    loads = []
+    for p in range(NPIECE):
+        rows = pl.ds(PIECE * (p % 2), PIECE)
+        loads.append(pltpu.make_async_copy(ints_hbm.at[p // 2, rows, :], ints.at[p % 3], i_sem.at[p]))
+    for load in loads[:3]:
         load.start()
 
     def remote(src, dst, send, recv, target):
@@ -103,7 +109,7 @@
         j = wrap(row + e - 1, NB)
         block = (occ[j, f].astype(jnp.float32) * occ_pat[f, j].astype(jnp.float32)).astype(bf)
         full = dot(dot(inner, block).astype(bf), inner, NT)
-        occ_mat[n] = jnp.where(same, full, 0.0).astype(bf)
+        occ_mat[n - 1] = jnp.where(same, full, 0.0).astype(bf)
         return 0
 
     lax.fori_loop(0, ND, lambda n, c: spread_occ(2 * n + 2, c), 0)
@@ -113,23 +119,23 @@
     eye = iota((W, W), 1) == owner * SUB + function
     ri_block = iota((1, W), 1) // PB
 
-    def turn(p, _):
+    def turn(p):
         e = p // 2
         keep = jnp.zeros((1, W), jnp.float32)
         for q in range(W // PB):
             value = ri[e, row, (W // PB) * col + q].astype(jnp.float32)
             keep = jnp.where(ri_block == q, value, keep)
         diag = jnp.where(eye, keep, 0.0).astype(bf)
-        lane = iota((1, PIECE), 1) + lax.rem(p, 2) * PIECE
+        lane = iota((1, PIECE), 1) + p % 2 * PIECE
         partner = sizes[wrap(row + e - 1, NB)]
         fill = jnp.where(((lane >> 5) < own_size) & ((lane & 31) < partner), 1.0, 0.0)
-        rows = ints[e, pl.ds(pl.multiple_of(lax.rem(p, 2) * PIECE, PIECE), PIECE), :]
-        right[p, 0:W, :] = (dot(diag, rows, NT) * fill).astype(bf)
-        return 0
-
-    for e in range(ND):
-        loads[e].wait()
-        lax.fori_loop(2 * e, 2 * e + 2, turn, 0)
+        right[p, 0:W, :] = (dot(diag, ints[p % 3], NT) * fill).astype(bf)
+
+    for p in range(NPIECE):
+        loads[p].wait()
+        turn(p)
+        if p + 3 < NPIECE:
+            loads[p + 3].start()
     pl.semaphore_wait(barrier, 8)
 
     def meet_signal(n, targets):
@@ -141,31 +147,31 @@
 
     meet_signal(0, y_dev)
 
-    def gather_copies(view, far, sems, targets):
+    def gather_copies(view, far_view, sems, targets):
         send, recv, on_send, on_recv = sems
         own, onward = {}, {}
         for way in (0, 1):
-            for p in range(NPIECE):
-                own[way, p] = remote(
-                    view(p, 1, 0, 0, W), view(p, 1, 1 + way, 0, W), send.at[way, p], recv.at[way, p], targets[way]
+            for q in range(NPIECE):
+                own[way, q] = remote(
+                    view(q, 1, 0, 0, W), view(q, 1, 1 + way, 0, W), send.at[way, q], recv.at[way, q], targets[way]
                 )
             for late in (0, 1):
                 part = 2 * late + way
-                for band in range(ND):
-                    onward[way, late, band] = remote(
-                        view(2 * band, 2, 1 + way, BASE[part], PART_ROWS[part]),
-                        far(2 * band, 2, part),
-                        on_send.at[way, late, band],
-                        on_recv.at[way, late, band],
+                for order in range(ND):
+                    onward[way, late, order] = remote(
+                        view(2 * order, 2, 1 + way, BASE[part], PART_ROWS[part]),
+                        far_view(2 * order, 2, part),
+                        on_send.at[way, late, order],
+                        on_recv.at[way, late, order],
                         targets[way],
                     )
         return own, onward
 
-    def right_view(p, n, slot, first, rows):
-        return right.at[pl.ds(p, n), pl.ds(QOFF[slot] + first, rows), :]
-
-    def right_far(p, n, part):
-        return right.at[pl.ds(p, n), pl.ds(QFAR[part], PART_ROWS[part]), :]
+    def right_view(q, n, slot, first, rows):
+        return right.at[pl.ds(2 * bands[q // 2] + q % 2, n), pl.ds(QOFF[slot] + first, rows), :]
+
+    def right_far(q, n, part):
+        return right.at[pl.ds(2 * bands[q // 2], n), pl.ds(QFAR[part], PART_ROWS[part]), :]
 
     def left_view(p, n, slot, first, rows):
         return left.at[pl.ds(p, n), slot, pl.ds(first, rows), :]
@@ -179,7 +185,6 @@
         for way in (0, 1):
             r_own[way, p].start()
 
-    near, far = 2 - 2 * k, 2 * k
     halos = {}
     for n, (band, target) in enumerate(((1, other), (near, other), (1, far_halo), (far, far_halo))):
         halos[n] = remote(mixed.at[band], halo.at[n], h_send.at[n], h_recv.at[n], target)
@@ -189,7 +194,7 @@
             h, start = g // 2, pl.multiple_of(lax.rem(g, 2) * LANES, LANES)
             total = None
             for e, f in pairs:
-                term = dot(right[2 * e + h, 0:W, pl.ds(start, LANES)], occ_mat[ND * e + f])
+                term = dot(right[2 * e + h, 0:W, pl.ds(start, LANES)], occ_mat[ND * e + f - 1])
                 total = term if total is None else total + term
             mixed[dm, :, pl.ds(pl.multiple_of(g * LANES, LANES), LANES)] = total.astype(bf)
             return 0
@@ -236,7 +241,6 @@
 
     meet_wait(0)
     meet_signal(1, z_dev)
-    bands = (near, far, 1)
     spread_vir(1)
     spread_vir(near)
     halos[0].wait_recv()
@@ -248,49 +252,56 @@
     halos[3].wait_recv()
     contract(2, ((mixed, 1, 1), (halo, 1, near), (halo, 3, far)))
 
-    for yy in (0, 1):
-        owner, function = function_of(iota((W, 1), 0))
-        target = iota((W, 8 * 128), 1)
-        one_hot[yy] = jnp.where(target == owner * 128 + yy * SUB + function, 1.0, 0.0).astype(bf)
+    owner, function = function_of(iota((W, 1), 0))
+    one_hot[...] = jnp.where(iota((W, 8 * 128), 1) == owner * 128 + function, 1.0, 0.0).astype(bf)
     lane = iota((1, NX * 128), 1)
     inside = lane & 127
     late = (inside >= SUB).astype(jnp.int32)
     column = (4 * late + (lane >> 7)) * SUB + inside - SUB * late
     place[...] = jnp.where((inside < 2 * SUB) & (iota(place.shape, 0) == column), 1.0, 0.0).astype(bf)
-    source = iota((NX * NX * SLOT, 1), 0)
+    source = iota((NX * SLOT, 1), 0)
     part = (source >> 4) & 3
     inside = source & 15
     target = (source >> 6) * SUB + PARTS[0] * part + inside
     real = inside < jnp.where(part == 3, PARTS[3], PARTS[0])
-    choose[...] = jnp.where(real & (iota(choose.shape, 1) == target), 1.0, 0.0).astype(bf)
+    for i, (n, yy) in enumerate(PLACES):
+        lane = iota(choose.shape[1:], 1) + (LANES * n - NX * SUB * yy)
+        choose[i] = jnp.where(real & (lane == target), 1.0, 0.0).astype(bf)
     for p in range(NPIECE):
         right[p, 1200:1280, :] = jnp.zeros((80, PIECE), bf)
         right[p, 1472:1536, :] = jnp.zeros((64, PIECE), bf)
         right[p, 1744:1792, :] = jnp.zeros((48, PIECE), bf)
     acc[W:, :] = jnp.zeros((acc.shape[0] - W, acc.shape[1]), jnp.float32)
-
-    def product(slot, first, lanes, rows=(0, W), orders=(0, 1, 2), add=False, into=0):
+    near_acc[2 * W :, :] = jnp.zeros((near_acc.shape[0] - 2 * W, near_acc.shape[1]), jnp.float32)
+
+    def product(slot, count, first, lanes, total, rows=(0, W), orders=(0, 1, 2), add=False, into=0):
         p_rows = pl.ds(rows[0], rows[1] - rows[0])
+        out_rows = p_rows if count == 1 else pl.ds(0, W * count)
+
+        def left_rows(piece):
+            if count == 1:
+                return left[piece, slot, p_rows, :]
+            return left[piece, slot : slot + count].reshape(count * W, PIECE)
 
         def body(n, _):
-            start = pl.multiple_of(into + n * LANES, LANES)
+            lane = pl.ds(pl.multiple_of(into + n * LANES, LANES), LANES)
             q_rows = pl.ds(pl.multiple_of(first + n * LANES, LANES), LANES)
-            total = acc[p_rows, pl.ds(start, LANES)] if add else None
+            value = total[out_rows, lane] if add else None
             for order in orders:
                 for h in (0, 1):
-                    term = dot(left[2 * order + h, slot, p_rows, :], right[2 * bands[order] + h, q_rows, :], NT)
-                    total = term if total is None else total + term
-            acc[p_rows, pl.ds(start, LANES)] = total
+                    term = dot(left_rows(2 * order + h), right[2 * bands[order] + h, q_rows, :], NT)
+                    value = term if value is None else value + term
+            total[out_rows, lane] = value
             return 0
 
         lax.fori_loop(0, lanes // LANES, body, 0)
 
-    def split(n, which, lane=0):
+    def split(n, which, total, row=0, lane=0):
         _, some, _, lanes, _ = GROUPS[n]
         for s in range(8):
             for i, part in enumerate(some):
-                first = BASE[part] + s * PARTS[part]
-                parts[n][s % 2, s // 2, which, TILE * i : TILE * i + TILE] = acc[first : first + TILE, lane : lane + lanes].astype(bf)
+                first = row + BASE[part] + s * PARTS[part]
+                parts[n][s % 2, s // 2, which, TILE * i : TILE * i + TILE] = total[first : first + TILE, lane : lane + lanes].astype(bf)
 
     core_copy, hop_copy = {}, {}
 
@@ -355,18 +366,25 @@
                 for q, lane, into, width in q_pieces:
                     there = wrap(y + (0, -1, 1, 2)[q])
                     block = total[i, :, lane - first : lane - first + width].astype(bf)
-                    fin[there, SLOT * slot + start : SLOT * slot + start + half, into : into + width] = block
+                    rows_in = pl.ds(SLOT * slot + start, half)
+                    fin[lax.rem(there, 2), there // 2, rows_in, into : into + width] = block
 
     exchange = {}
 
-    def exchange_start(n, slots):
-        rows = pl.ds(SLOT * slots[0], SLOT * len(slots))
-        for pair in (0, 1):
-            packed = dot(fin[2 * pair, rows, :], one_hot[0]) + dot(fin[2 * pair + 1, rows, :], one_hot[1])
-            packed = packed.astype(bf)
+    own_pair = y // 2
+
+    def exchange_start(n, first, count, pairs, some=None):
+        rows = pl.ds(first, count)
+        packed = None
+        for yy in (0, 1):
+            chunks = [fin[yy, pair, rows, :] for pair in pairs]
+            term = dot(chunks[0] if len(chunks) == 1 else jnp.concatenate(chunks, axis=0), one_hot[...])
+            packed = term if packed is None else packed + pltpu.roll(term, SUB, 1)
+        packed = packed.astype(bf)
+        for i, pair in enumerate(pairs):
             for s in range(8):
                 target = NX * (s // 2) + 2 * (s % 2) + pair
-                msgs[target, rows, :] = packed[:, 128 * s : 128 * s + 128]
+                msgs[target, rows, :] = packed[count * i : count * (i + 1), 128 * s : 128 * s + 128]
 
         def copy(m):
             target = NX * wrap(y + m // NX) + wrap(z + lax.rem(m, NX))
@@ -377,11 +395,17 @@
         exchange[n] = copy
 
         def begin(m, _):
-            copy(m).start()
+            if some is None:
+                copy(m).start()
+            else:
+
+                @pl.when(lax.rem(z + m, 2) == some)
+                def _():
+                    copy(m).start()
+
             return 0
 
         lax.fori_loop(1, NX * NX, begin, 0)
-        got[col, rows, :] = msgs[col, rows, :]
 
     def exchange_wait(n, what):
         def body(m, _):
@@ -394,98 +418,122 @@
         lax.fori_loop(1, NX * NX, body, 0)
 
     def arrive(order, own, onward):
-        for band in order:
+        for way in (0, 1):
+            own[way, 2 * order].wait_recv()
+            own[way, 2 * order + 1].wait_recv()
+            onward[way, 0, order].start()
+
+    def pass_late(onward):
+        for order in range(ND):
             for way in (0, 1):
-                own[way, 2 * band].wait_recv()
-                own[way, 2 * band + 1].wait_recv()
-                onward[way, 0, band].start()
-        for band in order:
+                onward[way, 1, order].start()
+
+    def far_arrive(onward, late, orders=(0, 1, 2)):
+        for order in orders:
             for way in (0, 1):
-                onward[way, 1, band].start()
-
-    def far_arrive(onward, late, order):
-        for band in order:
-            for way in (0, 1):
-                onward[way, late, band].wait_recv()
-
-    every = (0, 1, 2)
-    arrive(every, r_own, r_on)
-    product(0, 0, 1280)
-    split(0, 0)
+                onward[way, late, order].wait_recv()
+
+    for order in range(ND):
+        arrive(order, r_own, r_on)
+        if order == ND - 1:
+            pass_late(r_on)
+        product(0, 1, 0, 1280, acc, orders=(order,), add=order > 0)
+    split(0, 0, acc)
     core_start(0)
     meet_wait(1)
     meet_signal(2, z_dev)
-    stage1(0)
-    arrive(every, l_own, l_on)
-    product(1, 0, 1280)
-    split(1, 0)
+    for order in range(ND):
+        arrive(order, l_own, l_on)
+        if order == ND - 1:
+            pass_late(l_on)
+        product(1, 2, 0, 1280, near_acc, orders=(order,), add=order > 0)
+        if order == 0:
+            stage1(0)
+        if order == 1:
+            stage2(0)
+    split(1, 0, near_acc)
     core_start(1)
-    stage2(0)
-    product(2, 0, 1280)
-    split(2, 0)
+    split(2, 0, near_acc, W)
     core_start(2)
+    meet_wait(2)
     stage1(1)
-    meet_wait(2)
-    far_arrive(r_on, 0, every)
-    for i, slot in enumerate(every):
-        product(slot, 1280, 256)
-        split(3, i)
+    far_arrive(r_on, 0)
+    product(1, 2, 1280, 256, near_acc)
+    product(0, 1, 1280, 256, near_acc, into=256)
+    split(3, 0, near_acc, 0, 256)
+    split(3, 1, near_acc)
+    split(3, 2, near_acc, W)
     core_start(3)
     stage1(2)
     stage2(1)
     stage3(0)
-    early, late = (0, BASE[2]), (BASE[2], W)
     stage1(3)
     stage2(2)
-    far_arrive(l_on, 0, every)
-    product(3, 0, 1536, early)
+    early, late = (0, BASE[2]), (BASE[2], W)
+    far_arrive(l_on, 0)
+    product(3, 1, 0, 1536, acc, early)
     stage3(1)
     stage2(3)
-    far_arrive(r_on, 1, every)
-    product(3, 1536, 256, early, into=1536)
-    split(5, 0)
+    far_arrive(r_on, 1)
+    product(3, 1, 1536, 256, acc, early, into=1536)
+    split(5, 0, acc)
     core_start(5)
-    for i, slot in enumerate(every):
-        product(slot, 1536, 256, into=1536)
-        split(4, i, 1536)
+    product(1, 2, 1536, 256, near_acc)
+    product(0, 1, 1536, 256, near_acc, into=256)
+    split(4, 0, near_acc, 0, 256)
+    split(4, 1, near_acc)
+    split(4, 2, near_acc, W)
     core_start(4)
     stage1(5)
     stage3(2)
     far_arrive(l_on, 1, (0,))
-    product(3, 0, 1792, late, (0,))
+    product(3, 1, 0, 1792, acc, late, (0,))
     stage1(4)
     stage3(3)
     stage2(5)
     far_arrive(l_on, 1, (1,))
-    product(3, 0, 1792, late, (1,), True)
+    product(3, 1, 0, 1792, acc, late, (1,), True)
     stage2(4)
+    exchange_start(0, 0, 3 * SLOT, (own_pair,), own_pair)
     far_arrive(l_on, 1, (2,))
-    product(3, 0, 1792, late, (2,), True)
-    split(6, 0)
+    product(3, 1, 0, 1792, acc, late, (2,), True)
+    split(6, 0, acc)
     core_start(6)
     stage3(5)
     stage3(4)
     stage1(6)
-    exchange_start(0, every)
+    exchange_start(0, 0, 3 * SLOT, (1 - own_pair,), 1 - own_pair)
     stage2(6)
+    exchange_start(1, 3 * SLOT, SLOT // 2, (0, 1))
     stage3(6)
-    exchange_start(1, (3,))
-
-    for n in (0, 1):
+    exchange_start(2, 3 * SLOT + SLOT // 2, SLOT // 2, (0, 1))
+    got[col] = msgs[col]
+
+    for n in (0, 1, 2):
         exchange_wait(n, "recv")
     slot_of = {0: 0, 3: 1, 1: 2, 2: 3}
+    for copy in halos.values():
+        copy.wait_send()
+    wide = mixed.at[0]
     for yy in range(NX):
         rows = [
             jnp.concatenate([got[NX * yy + src, pl.ds(SLOT * slot_of[(zz - src) % NX], SLOT)] for src in range(NX)], axis=1)
             for zz in range(NX)
         ]
         wide[:, 256 * yy : 256 * yy + 256] = dot(place[...], jnp.concatenate(rows, axis=0), NT).astype(bf)
-    out[...] = dot(wide[...], choose[...]).astype(bf)
-
-    for copies in (r_own, r_on, l_own, l_on, halos, core_copy, hop_copy):
+    for n in range(4):
+        width = min(LANES, 800 - LANES * n)
+        total = None
+        for i, (tile, yy) in enumerate(PLACES):
+            if tile == n:
+                term = dot(wide[:, 256 * yy : 256 * yy + 256], choose[i, :, 0:width])
+                total = term if total is None else total + term
+        out[:, LANES * n : LANES * n + width] = total.astype(bf)
+
+    for copies in (r_own, r_on, l_own, l_on, core_copy, hop_copy):
         for copy in copies.values():
             copy.wait_send()
-    for n in (0, 1):
+    for n in (0, 1, 2):
         exchange_wait(n, "send")
 
 
@@ -497,32 +545,32 @@
     dma = pltpu.SemaphoreType.DMA
     shapes = [(len(slots), TILE * len(some), lanes) for slots, some, _, lanes, _ in GROUPS]
     scratch = [
-        pltpu.VMEM((ND, BLK * BLK, W), bf),
+        pltpu.VMEM((3, PIECE, W), bf),
         pltpu.VMEM((NPIECE, QROWS, PIECE), bf),
         pltpu.VMEM((NPIECE, NX, W, PIECE), bf),
         pltpu.VMEM((ND, W, BLK * BLK), bf),
         pltpu.VMEM((4, W, BLK * BLK), bf),
-        pltpu.VMEM((ND * ND, LANES, LANES), bf),
+        pltpu.VMEM((ND * ND - 2, LANES, LANES), bf),
         pltpu.VMEM((ND, BLK * BLK, BLK * BLK), bf),
         pltpu.VMEM((BLK, BLK * BLK), jnp.float32),
         pltpu.VMEM((BLK, BLK * BLK), jnp.float32),
         pltpu.VMEM((416, QROWS), jnp.float32),
-        pltpu.VMEM((NX, NX * SLOT, W), bf),
-        pltpu.VMEM((2, W, 8 * 128), bf),
+        pltpu.VMEM((2 * W + 16, 1280), jnp.float32),
+        pltpu.VMEM((2, 2, NX * SLOT, W), bf),
+        pltpu.VMEM((W, 8 * 128), bf),
         pltpu.VMEM((W, NX * 128), bf),
-        pltpu.VMEM((NX * NX * SLOT, 800), bf),
-        pltpu.VMEM((W, NX * NX * SLOT), bf),
+        pltpu.VMEM((len(PLACES), LANES, LANES), bf),
         pltpu.VMEM((NX * NX, NX * SLOT, 128), bf),
         pltpu.VMEM((NX * NX, NX * SLOT, 128), bf),
         *[pltpu.VMEM((2, NX, n, rows, lanes), bf) for n, rows, lanes in shapes],
         *[pltpu.VMEM((NX, n, rows, lanes), bf) for n, rows, lanes in shapes],
         *[pltpu.VMEM((2, 3, n, rows // 2, lanes), bf) for n, rows, lanes in shapes],
-        dma((ND,)),
+        dma((NPIECE,)),
         *[dma((2, NPIECE)), dma((2, NPIECE)), dma((2, 2, ND)), dma((2, 2, ND))] * 2,
         dma((4,)), dma((4,)),
         dma((NG,)), dma((NG,)),
         dma((NG, 2, 3)), dma((NG, 2, 3)),
-        dma((2, NX * NX - 1)), dma((2, NX * NX - 1)),
+        dma((3, NX * NX - 1)), dma((3, NX * NX - 1)),
         pltpu.SemaphoreType.REGULAR((3,)),
     ]
     response = pl.pallas_call(

time: 132 us -> 127 us (0.962)
  Pallas kernels: 129 us -> 125 us
    pallas_call x1, Pallas kernels: 129 us -> 125 us  [local(): pl.pallas_call(kernel, out_shape=jax.ShapeDtypeStruct((W, 800), bf), in_s...]
where the time goes in v4:
time: 127 us
  Pallas kernels  125 us (98%)
  other arithmetic  2.3 us (2%)
    pallas_call x1, Pallas kernels, local(): pl.pallas_call(kernel, out_shape=jax.ShapeDtypeStruct((W, 800), bf), in_s...  125 us

profile of v4, /device:TPU:0, one launch (start us, length us, event | category | flops | bytes accessed | tf_op | source)
XLA Modules:
  0.0 127.3 jit_solution(5645925102304464786)
XLA Ops:
  0.0 125.0 %shard_map.73 = bf16[400,800]{1,0:T(8,128)(2,1)} custom-call(s32[8]{0:T(128)} %sizes.1, s32[3,8,64]{2,1,0:T(8,128)} %bitcast.7, s32[3,8]{1,0:T(4,128)} %bitcast.8, s32[3,8]{1,0:T(4,128)} %bitcast.9, bf16[3,1024,400]{2,1,0:T(8,128)(2,1)} %bitcast.6, bf16[8,3,32,32]{3,2,1,0:T(8,128)(2,1)} %occ.1, bf16[8,3,32,32]{3,2,1,0:T(8,128)(2,1)} %vir.1), custom_call_target="tpu_custom_call" | custom-call | tf_op jit(solution)/shard_map/pallas_call | solution.py:576
  125.0 2.3 %convert_bitcast_fusion = f32[800,400]{0,1:T(8,128)} fusion(bf16[400,800]{1,0:T(8,128)(2,1)} %shard_map.73), kind=kLoop, calls=%fused_computation | loop fusion | flops 320000 | bytes 1920000 | tf_op jit(solution)/shard_map/transpose | solution.py:586

commit v5 on v4

--- a/solution.py
+++ b/solution.py
@@ -39,6 +39,7 @@
     ((3,), (2, 3), 0, 1792, (*NEAR, FAR_A, FAR_B)),
 )
 NG = len(GROUPS)
+FAR_FIRST = (10, 6, 14, 9, 11, 2, 8, 5, 7, 13, 15, 1, 3, 4, 12)
 PLACES = ((0, 0), (0, 1), (1, 1), (1, 2), (2, 2), (2, 3), (3, 3))
 
 
@@ -119,21 +120,25 @@
     eye = iota((W, W), 1) == owner * SUB + function
     ri_block = iota((1, W), 1) // PB
 
-    def turn(p):
-        e = p // 2
+    def keep_of(e):
         keep = jnp.zeros((1, W), jnp.float32)
         for q in range(W // PB):
             value = ri[e, row, (W // PB) * col + q].astype(jnp.float32)
             keep = jnp.where(ri_block == q, value, keep)
-        diag = jnp.where(eye, keep, 0.0).astype(bf)
+        return jnp.where(eye, keep, 0.0).astype(bf)
+
+    def turn(p, diag):
         lane = iota((1, PIECE), 1) + p % 2 * PIECE
-        partner = sizes[wrap(row + e - 1, NB)]
+        partner = sizes[wrap(row + p // 2 - 1, NB)]
         fill = jnp.where(((lane >> 5) < own_size) & ((lane & 31) < partner), 1.0, 0.0)
         right[p, 0:W, :] = (dot(diag, ints[p % 3], NT) * fill).astype(bf)
 
+    diag = None
     for p in range(NPIECE):
+        if p % 2 == 0:
+            diag = keep_of(p // 2)
         loads[p].wait()
-        turn(p)
+        turn(p, diag)
         if p + 3 < NPIECE:
             loads[p + 3].start()
     pl.semaphore_wait(barrier, 8)
@@ -207,8 +212,6 @@
     lax.fori_loop(0, 4, lambda n, c: spread_occ(2 * n + 1, c), 0)
     mix(near, ((near // 2, near + 1 - near // 2), (near // 2 + 1, near - near // 2)))
     halos[1].start()
-    mix(far, ((far // 2, far + 1 - far // 2), (far // 2 + 1, far - far // 2)))
-    halos[3].start()
 
     match[...] = jnp.where(iota(match.shape, 0) == (iota(match.shape, 1) & 31), 1.0, 0.0)
     repeat = ((iota((BLK, BLK * BLK), 1) >> 5) == iota((BLK, BLK * BLK), 0)).astype(bf)
@@ -225,17 +228,12 @@
         lax.fori_loop(0, BLK, body, 0)
 
     def contract(order, terms):
-        def body(h, _):
-            columns = pl.ds(pl.multiple_of(h * PIECE, PIECE), PIECE)
+        for h in (0, 1):
             total = None
             for ref, index, g in terms:
-                term = dot(ref[index], vir_mat[g, :, columns])
+                term = dot(ref[index], vir_mat[g, :, PIECE * h : PIECE * (h + 1)])
                 total = term if total is None else total + term
             left[2 * order + h, 0] = total.astype(bf)
-            return 0
-
-        lax.fori_loop(0, 2, body, 0)
-        for h in (0, 1):
             for way in (0, 1):
                 l_own[way, 2 * order + h].start()
 
@@ -245,6 +243,8 @@
     spread_vir(near)
     halos[0].wait_recv()
     contract(0, ((mixed, near, 1), (halo, 0, near)))
+    mix(far, ((far // 2, far + 1 - far // 2), (far // 2 + 1, far - far // 2)))
+    halos[3].start()
     spread_vir(far)
     halos[2].wait_recv()
     contract(1, ((mixed, far, 1), (halo, 2, far)))
@@ -394,28 +394,18 @@
 
         exchange[n] = copy
 
-        def begin(m, _):
+        for m in FAR_FIRST:
             if some is None:
                 copy(m).start()
             else:
-
-                @pl.when(lax.rem(z + m, 2) == some)
-                def _():
-                    copy(m).start()
-
-            return 0
-
-        lax.fori_loop(1, NX * NX, begin, 0)
+                pl.when(lax.rem(z + m, 2) == some)(copy(m).start)
 
     def exchange_wait(n, what):
-        def body(m, _):
+        for m in FAR_FIRST:
             if what == "recv":
                 exchange[n](m).wait_recv()
             else:
                 exchange[n](m).wait_send()
-            return 0
-
-        lax.fori_loop(1, NX * NX, body, 0)
 
     def arrive(order, own, onward):
         for way in (0, 1):
@@ -499,17 +489,16 @@
     product(3, 1, 0, 1792, acc, late, (2,), True)
     split(6, 0, acc)
     core_start(6)
+    stage1(6)
     stage3(5)
     stage3(4)
-    stage1(6)
     exchange_start(0, 0, 3 * SLOT, (1 - own_pair,), 1 - own_pair)
     stage2(6)
-    exchange_start(1, 3 * SLOT, SLOT // 2, (0, 1))
     stage3(6)
-    exchange_start(2, 3 * SLOT + SLOT // 2, SLOT // 2, (0, 1))
+    exchange_start(1, 3 * SLOT, SLOT, (0, 1))
     got[col] = msgs[col]
 
-    for n in (0, 1, 2):
+    for n in (0, 1):
         exchange_wait(n, "recv")
     slot_of = {0: 0, 3: 1, 1: 2, 2: 3}
     for copy in halos.values():
@@ -533,7 +522,7 @@
     for copies in (r_own, r_on, l_own, l_on, core_copy, hop_copy):
         for copy in copies.values():
             copy.wait_send()
-    for n in (0, 1, 2):
+    for n in (0, 1):
         exchange_wait(n, "send")
 
 
@@ -570,7 +559,7 @@
         dma((4,)), dma((4,)),
         dma((NG,)), dma((NG,)),
         dma((NG, 2, 3)), dma((NG, 2, 3)),
-        dma((3, NX * NX - 1)), dma((3, NX * NX - 1)),
+        dma((2, NX * NX - 1)), dma((2, NX * NX - 1)),
         pltpu.SemaphoreType.REGULAR((3,)),
     ]
     response = pl.pallas_call(

time: 127 us -> 127 us (level)
  no operation moved by 1% of the time
where the time goes in v5:
time: 127 us; the launch traced here: 126 us
  Pallas kernels  124 us (98%)
  other arithmetic  2.3 us (2%)
    pallas_call x1, Pallas kernels, local(): pl.pallas_call(kernel, out_shape=jax.ShapeDtypeStruct((W, 800), bf), in_s...  124 us

profile of v5, /device:TPU:0, one launch (start us, length us, event | category | flops | bytes accessed | tf_op | source)
XLA Modules:
  0.0 126.3 jit_solution(1219371810851947532)
XLA Ops:
  0.0 124.0 %shard_map.73 = bf16[400,800]{1,0:T(8,128)(2,1)} custom-call(s32[8]{0:T(128)} %sizes.1, s32[3,8,64]{2,1,0:T(8,128)} %bitcast.7, s32[3,8]{1,0:T(4,128)} %bitcast.8, s32[3,8]{1,0:T(4,128)} %bitcast.9, bf16[3,1024,400]{2,1,0:T(8,128)(2,1)} %bitcast.6, bf16[8,3,32,32]{3,2,1,0:T(8,128)(2,1)} %occ.1, bf16[8,3,32,32]{3,2,1,0:T(8,128)(2,1)} %vir.1), custom_call_target="tpu_custom_call" | custom-call | tf_op jit(solution)/shard_map/pallas_call | solution.py:565
  124.0 2.3 %convert_bitcast_fusion = f32[800,400]{0,1:T(8,128)} fusion(bf16[400,800]{1,0:T(8,128)(2,1)} %shard_map.73), kind=kLoop, calls=%fused_computation | loop fusion | flops 320000 | bytes 1920000 | tf_op jit(solution)/shard_map/transpose | solution.py:575

commit v6 on v5

--- a/solution.py
+++ b/solution.py
@@ -475,12 +475,12 @@
     split(4, 2, near_acc, W)
     core_start(4)
     stage1(5)
+    stage1(4)
     stage3(2)
     far_arrive(l_on, 1, (0,))
     product(3, 1, 0, 1792, acc, late, (0,))
-    stage1(4)
+    stage2(5)
     stage3(3)
-    stage2(5)
     far_arrive(l_on, 1, (1,))
     product(3, 1, 0, 1792, acc, late, (1,), True)
     stage2(4)

time: 127 us -> 127 us (level)
  no operation moved by 1% of the time
where the time goes in v6:
time: 127 us; the launch traced here: 126 us
  Pallas kernels  124 us (98%)
  other arithmetic  2.3 us (2%)
    pallas_call x1, Pallas kernels, local(): pl.pallas_call(kernel, out_shape=jax.ShapeDtypeStruct((W, 800), bf), in_s...  124 us

profile of v6, /device:TPU:0, one launch (start us, length us, event | category | flops | bytes accessed | tf_op | source)
XLA Modules:
  0.0 126.4 jit_solution(1616458928417282515)
XLA Ops:
  0.0 124.1 %shard_map.73 = bf16[400,800]{1,0:T(8,128)(2,1)} custom-call(s32[8]{0:T(128)} %sizes.1, s32[3,8,64]{2,1,0:T(8,128)} %bitcast.7, s32[3,8]{1,0:T(4,128)} %bitcast.8, s32[3,8]{1,0:T(4,128)} %bitcast.9, bf16[3,1024,400]{2,1,0:T(8,128)(2,1)} %bitcast.6, bf16[8,3,32,32]{3,2,1,0:T(8,128)(2,1)} %occ.1, bf16[8,3,32,32]{3,2,1,0:T(8,128)(2,1)} %vir.1), custom_call_target="tpu_custom_call" | custom-call | tf_op jit(solution)/shard_map/pallas_call | solution.py:565
  124.1 2.3 %convert_bitcast_fusion = f32[800,400]{0,1:T(8,128)} fusion(bf16[400,800]{1,0:T(8,128)(2,1)} %shard_map.73), kind=kLoop, calls=%fused_computation | loop fusion | flops 320000 | bytes 1920000 | tf_op jit(solution)/shard_map/transpose | solution.py:575
